TPU v7x, 512 devices: a whole 4x4x16 slice. The times are simulated.
512 devices in a mesh: dp: 64 (over y, z), tensor: 8 (over x, core).
Axes of the slice: x: 4, y: 4, z: 16, core: 2. Of those that a mesh axis runs over, the one named last changes fastest.
Arguments:
- normed: bfloat16 [23552, 4096], P('dp', 'tensor'), may hold values from -6 to 6
- kv_cotangent: bfloat16 [2, 23552, 1024], P(None, 'dp', 'tensor'), may hold values from -6 to 6
- kv_weight: bfloat16 [2, 4096, 1024], P(None, 'dp', 'tensor'), may hold values from -0.25 to 0.25
- error_buffer: bfloat16 [64, 2, 4096, 1024], P('dp', None, None, 'tensor'), may hold values from -383.66652 to 383.66652
- q_factor: float32 [2, 16, 1024], P(None, None, 'tensor'), may hold values from -40 to 40
Outputs:
- input_grad: bfloat16 [23552, 4096], P('dp', 'tensor')
- approx: bfloat16 [2, 4096, 1024], P(None, 'dp', 'tensor')
- new_error: bfloat16 [64, 2, 4096, 1024], P('dp', None, None, 'tensor')
All inputs are finite; a program needn't handle non-finite values.
Results may differ from a plain program's by a relative error of at most 0.018.
Values may be sent and summed in bfloat16 or wider, within the bound.
No kernel may reach another device: no remote copies, remote signals or barrier semaphores. Data moves between devices by JAX's collectives and lax.ppermute only.
A program may use at most 64 MiB of HBM per device.

v0:
```python
import jax
import jax.numpy as jnp
from jax import lax
from jax.sharding import PartitionSpec as P

EPSILON = 1e-06


def unchanged(values):
    return values


def orthonormal(p_sum, total_fn):
    highest = lax.Precision.HIGHEST

    def column_step(column, basis_cols):
        vector = lax.dynamic_index_in_dim(p_sum, column, 1, keepdims=False)
        coeffs = total_fn(jnp.einsum("kid,kd->ki", basis_cols, vector, precision=highest))
        vector = vector - jnp.einsum("ki,kid->kd", coeffs, basis_cols, precision=highest)
        length = jnp.sqrt(total_fn(jnp.sum(vector * vector, axis=-1)) + EPSILON)
        return lax.dynamic_update_index_in_dim(basis_cols, vector / length[:, None], column, 1)

    return lax.fori_loop(0, p_sum.shape[1], column_step, jnp.zeros_like(p_sum))


def shards(normed, kv_cotangent, kv_weight, error_buffer, q_factor):
    highest = lax.Precision.HIGHEST
    workers = lax.axis_size("dp")
    gradient = jnp.einsum(
        "td,ktc->kdc",
        lax.all_gather(normed, "tensor", axis=1, tiled=True),
        kv_cotangent,
        preferred_element_type=jnp.float32,
    )
    moment = gradient + error_buffer[0].astype(jnp.float32)
    factor_term = jnp.einsum("kdc,krc->krd", moment, q_factor, precision=highest) / workers
    whole_sum = lax.psum(factor_term, ("dp", "tensor"))
    basis_cols = orthonormal(whole_sum, unchanged)
    q_term = jnp.einsum("krd,kdc->krc", basis_cols, moment, precision=highest) / workers
    q_total = lax.psum(q_term, "dp")
    approx_full = jnp.einsum("krd,krc->kdc", basis_cols, q_total, precision=highest)
    new_error = (moment - approx_full).astype(jnp.bfloat16)[None]
    row_count = approx_full.shape[1] // workers
    approx_rows = lax.dynamic_slice_in_dim(
        approx_full, lax.axis_index("dp") * row_count, row_count, 1
    ).astype(jnp.bfloat16)
    partial_value = jnp.einsum(
        "ktc,kdc->td",
        kv_cotangent,
        lax.all_gather(kv_weight, "dp", axis=1, tiled=True),
        preferred_element_type=jnp.float32,
    )
    input_grad = lax.psum_scatter(
        partial_value.astype(jnp.bfloat16), "tensor", scatter_dimension=1, tiled=True
    )
    return (input_grad, approx_rows, new_error)


def solution(mesh):
    in_specs = (
        P("dp", "tensor"),
        P(None, "dp", "tensor"),
        P(None, "dp", "tensor"),
        P("dp", None, None, "tensor"),
        P(None, None, "tensor"),
    )
    out_specs = (P("dp", "tensor"), P(None, "dp", "tensor"), P("dp", None, None, "tensor"))
    return jax.shard_map(shards, mesh=mesh, in_specs=in_specs, out_specs=out_specs, check_vma=False)
```

profile of v0, /device:TPU:2, one launch (start us, length us, event | category | flops | bytes accessed | tf_op | source)
XLA Modules:
  0.0 1006.5 jit_solution(17631461177154050979)
XLA Ops:
  8.7 2.9 copy.8
  11.7 36.9 %all-gather.5.cloned.1.call-done = bf16[368,4096]{1,0:T(8,128)(2,1)} async-done(((bf16[368,512]{1,0:T(8,128)(2,1)}), bf16[368,4096]{1,0:T(8,128)(2,1)}) %all-gather.5.cloned.1.call-update) | async-done | bytes 3014672 | tf_op jit(solution)/shard_map/all_gather | solution.py:31
  48.6 3.1 fusion.1
  51.8 1.9 copy-done.1
  53.7 3.1 fusion.2
  56.9 136.9 %all-gather.3.cloned.1.call-done = bf16[2,4096,128]{2,1,0:T(8,128)(2,1)} async-done(((bf16[2,64,128]{2,1,0:T(8,128)(2,1)}), bf16[2,4096,128]{2,1,0:T(8,128)(2,1)}) %all-gather.3.cloned.1.call-update) | async-done | bytes 2097168 | tf_op jit(solution)/shard_map/all_gather | solution.py:50
  193.8 4.2 bitcast_convert_fusion
  198.0 457.0 %all-reduce.2.cloned.1.call-done = f32[2,16,4096]{2,1,0:T(8,128)} async-done(((f32[2,16,4096]{2,1,0:T(8,128)}), f32[2,16,4096]{2,1,0:T(8,128)}) %all-reduce.2.cloned.1.call-update) | async-done | bytes 524304 | tf_op jit(solution)/shard_map/psum | solution.py:37
  655.0 41.2 %while.13 = (s32[]{:T(128)}, f32[2,16,4096]{2,1,0:T(8,128)S(1)}, f32[2,16,4096]{2,1,0:T(8,128)}, s32[]{:T(128)}, s32[]{:T(128)}) while((s32[]{:T(128)}, f32[2,16,4096]{2,1,0:T(8,128)S(1)}, f32[2,16,4096]{2,1,0:T(8,128)}, s32[]{:T(128)}, s32[]{:T(128)}) %tuple.34), condition=%wide.region_4.5_spmd, body=%wide.region_2.4_spmd.sunk | while | flops 3186690 | bytes 1540453 | solution.py:23
  670.5 1.0 constant_dynamic-slice_fusion.2
  673.1 1.0 constant_dynamic-slice_fusion.2
  678.2 1.0 constant_dynamic-slice_fusion.2
  680.8 1.0 constant_dynamic-slice_fusion.2
  683.4 1.0 constant_dynamic-slice_fusion.2
  685.9 1.0 constant_dynamic-slice_fusion.2
  688.5 1.0 constant_dynamic-slice_fusion.2
  693.7 1.0 constant_dynamic-slice_fusion.2
  696.2 5.1 convolution_multiply_fusion.1
  701.3 276.9 %psum.15 = f32[2,16,128]{2,1,0:T(8,128)S(1)} all-reduce(f32[2,16,128]{2,1,0:T(8,128)S(1)} %convolution_multiply_fusion.1), channel_id=1, replica_groups=mesh['dp'=64,'tensor'=8] {'dp'}, use_global_device_ids=true, to_apply=%region_5.6 | all-reduce | flops 4096 | bytes 32768 | tf_op jit(solution)/shard_map/psum | solution.py:40
  978.2 8.2 fusion.6
  986.4 5.7 copy.11
  992.1 4.0 fusion.4
  996.1 2.5 copy.12
  998.5 1.5 dynamic-slice_convert_fusion
  (151 shorter events, 34.0 us)
Async XLA Ops:
  7.2 41.4 %copy-start = (bf16[2,368,128]{2,1,0:T(8,128)(2,1)S(1)}, bf16[2,368,128]{2,1,0:T(8,128)(2,1)}, u32[]{:S(2)}) copy-start(bf16[2,368,128]{2,1,0:T(8,128)(2,1)} %param.8) | copy-start | bytes 565252
  7.2 41.4 %all-gather.5.cloned.1.call-start = ((), (), s32[]{:S(2)}) async-start(), calls=%async_computation.3 | async-start | bytes 3391488 | tf_op jit(solution)/shard_map/all_gather | solution.py:31
  7.9 185.9 %all-gather.3.cloned.1.call-start = ((), (), s32[]{:S(2)}) async-start(), calls=%async_computation.1 | async-start | bytes 2129920 | tf_op jit(solution)/shard_map/all_gather | solution.py:50
  8.7 646.3 %all-reduce.2.cloned.1.call-start = ((), (), s32[]{:S(2)}) async-start(), calls=%async_computation.4 | async-start | bytes 1048576 | tf_op jit(solution)/shard_map/psum | solution.py:37
  11.7 42.0 %copy-start.2 = (f32[2,16,128]{2,1,0:T(8,128)S(1)}, f32[2,16,128]{2,1,0:T(8,128)}, u32[]{:S(2)}) copy-start(f32[2,16,128]{2,1,0:T(8,128)} %param.11) | copy-start | bytes 49156
  51.8 1.9 copy-start.1
  56.8 943.2 %reduce-scatter.2.cloned.1.call-start = ((), (), s32[]{:S(2)}) async-start(), calls=%async_computation.2 | async-start | bytes 3391488 | tf_op jit(solution)/shard_map/reduce_scatter | solution.py:53
Sparse Core Ops, SparseCore 0:
  10.1 38.4 all-gather.4
  51.6 142.2 all-gather.2
  199.8 455.1 all-reduce.1
  658.5 35.6 reduce-scatter.1
where the time goes:
time: 1010 us
  waiting for transfers between devices  632 us (63%)
  blocking collectives  277 us (27%)
  matrix products  40.8 us (4%)
  local copies, waits for them, and re-layouts  33.6 us (3%)
  between operations  13.8 us (1%)
    psum x1, waiting for transfers between devices, shards(): whole_sum = lax.psum(factor_term, ('dp', 'tensor'))  457 us
    psum x1, blocking collectives, shards(): q_total = lax.psum(q_term, 'dp')  277 us
    all_gather x1, waiting for transfers between devices, shards(): lax.all_gather(kv_weight, 'dp', axis=1, tiled=True)  137 us
    all_gather x1, waiting for transfers between devices, shards(): lax.all_gather(normed, 'tensor', axis=1, tiled=True)  36.9 us
  transfers between devices with their start and end apart: 4, of which 3 were waited for; matrix products, arithmetic and copies ran while one was open for 8% of the time, Pallas kernels for 0%

commit v1 on v0

v1 whole, which is shorter than its diff:
```python
import jax
import jax.numpy as jnp
from jax import lax
from jax.experimental import pallas as pl
from jax.experimental.pallas import tpu as pltpu
from jax.sharding import Mesh
from jax.sharding import PartitionSpec as P

EPSILON = 1e-06
WORKERS = 64
NY, NZ, NX, NC = 4, 16, 4, 2
NT = NX * NC
RANK = 16
ROWS = 2 * RANK
D = 4096
BLK = D // NT
TOK = 368
TOKP = 384
COL = 128
GCOL = BLK + 2 * COL
F32 = jnp.float32
BF16 = jnp.bfloat16
VMEM = pl.BlockSpec(memory_space=pltpu.VMEM)
SMEM = pl.BlockSpec(memory_space=pltpu.SMEM)
NT_DIMS = (((1,), (1,)), ((), ()))
NN_DIMS = (((1,), (0,)), ((), ()))
TN_DIMS = (((0,), (0,)), ((), ()))


def dot(a, b, dims):
    return lax.dot_general(a, b, dims, preferred_element_type=F32)


def pieces(value, count):
    result = []
    for _ in range(count):
        part = value.astype(BF16)
        result.append(part)
        value = value - part.astype(F32)
    return result


def call(kernel, out_shape, *args, scratch=(), specs=None, flops=0, moved=0):
    outs = jax.tree.map(lambda _: VMEM, out_shape)
    return pl.pallas_call(
        kernel,
        out_shape=out_shape,
        in_specs=specs or [VMEM] * len(args),
        out_specs=outs,
        scratch_shapes=list(scratch),
        compiler_params=pltpu.CompilerParams(vmem_limit_bytes=24 * 2**20),
        cost_estimate=pl.CostEstimate(flops=flops, bytes_accessed=moved, transcendentals=0),
    )(*args)


def shape(dims, dtype=F32):
    return jax.ShapeDtypeStruct(dims, dtype)


def first_kernel(error_ref, cot_ref, q_ref, out_ref):
    out_ref[:, :, BLK + TOKP - 128 :] = jnp.zeros((NT, ROWS, 128), F32)
    for k in range(2):
        rows = slice(RANK * k, RANK * (k + 1))
        q = jnp.concatenate(pieces(q_ref[k], 3), axis=0)
        token = dot(q, cot_ref[k], NT_DIMS)
        token = token[:RANK] + token[RANK : 2 * RANK] + token[2 * RANK :]
        for t in range(NT):
            part = dot(q, error_ref[k, BLK * t : BLK * (t + 1), :], NT_DIMS)
            out_ref[t, rows, :BLK] = part[:RANK] + part[RANK : 2 * RANK] + part[2 * RANK :]
            out_ref[t, rows, BLK : BLK + TOK] = token


def second_kernel(recv_ref, normed_ref, weight_ref, out_ref):
    total = recv_ref[0]
    for t in range(1, NT):
        total = total + recv_ref[t]
    token = jnp.concatenate(pieces(total[:, BLK : BLK + TOK], 3), axis=0)
    grad = dot(token, normed_ref[...], NN_DIMS)
    factor = total[:, :BLK] + (grad[:ROWS] + grad[ROWS : 2 * ROWS] + grad[2 * ROWS :])
    weight = jnp.concatenate([weight_ref[0], weight_ref[1]], axis=1).astype(F32)
    weight = jnp.concatenate([weight[:32], weight[32:]], axis=1)
    for y in range(NY):
        out_ref[y, :8, :] = factor[8 * y : 8 * y + 8]
        out_ref[y, 8:, :] = weight


def third_kernel(recv_ref, out_ref, weight_ref):
    total = (recv_ref[0, :8] + recv_ref[1, :8]) + (recv_ref[2, :8] + recv_ref[3, :8])
    for z in range(NZ):
        out_ref[z] = total
    for y in range(NY):
        weight = recv_ref[y, 8:, :]
        weight_ref[y] = jnp.concatenate([weight[:, :256], weight[:, 256:]], axis=0).astype(BF16)


def repeat_kernel(scale, recv_ref, out_ref):
    total = recv_ref[0]
    for i in range(1, recv_ref.shape[0]):
        total = total + recv_ref[i]
    total = total * scale
    for i in range(out_ref.shape[0]):
        out_ref[i] = total


def basis_kernel(recv_ref, gathered_ref, cot_ref, error_ref, basis_ref, term_ref, p_ref, v_ref):
    for y in range(NY):
        for t in range(NT):
            block = recv_ref[NT * y + t]
            p_ref[8 * y : 8 * y + 8, BLK * t : BLK * (t + 1)] = block
            v_ref[8 * y : 8 * y + 8, BLK * t : BLK * (t + 1)] = block
    for i in range(RANK):
        for k in range(2):
            row = RANK * k + i
            vector = v_ref[row : row + 1, :]
            square = jnp.sum(vector * vector, axis=1, keepdims=True) + EPSILON
            inverse = 1.0 / jnp.sqrt(square)
            column = vector * inverse
            basis_ref[row : row + 1, :] = column
            if i < RANK - 1:
                low = RANK * k + 8 * ((i + 1) // 8)
                rows = slice(low, RANK * (k + 1))
                coeff = jnp.sum(p_ref[rows, :] * column, axis=1, keepdims=True)
                v_ref[rows, :] = v_ref[rows, :] - coeff * column
    basis = [jnp.concatenate(pieces(basis_ref[RANK * k : RANK * (k + 1), :], 3), axis=0) for k in range(2)]
    both = jnp.concatenate(basis, axis=0)
    token = jnp.zeros((96, TOK), F32)
    for t in range(NT):
        token = token + dot(
            both[:, BLK * t : BLK * (t + 1)], gathered_ref[:, GCOL * t : GCOL * t + BLK], NT_DIMS
        )
    for k in range(2):
        reduced = token[48 * k : 48 * k + 16] + token[48 * k + 16 : 48 * k + 32] + token[48 * k + 32 : 48 * k + 48]
        reduced = jnp.concatenate(pieces(reduced, 3), axis=0)
        term = dot(reduced, cot_ref[k], NN_DIMS) + dot(basis[k], error_ref[k], NN_DIMS)
        term = term[:RANK] + term[RANK : 2 * RANK] + term[2 * RANK :]
        for z in range(NZ):
            term_ref[z, RANK * k : RANK * (k + 1), :] = term


def final_kernel(worker_ref, recv_ref, basis_ref, gathered_ref, cot_ref, error_ref, approx_ref, new_ref, tile_ref):
    q_total = (recv_ref[0] + recv_ref[1]) + (recv_ref[2] + recv_ref[3])
    q_total = q_total * (1.0 / WORKERS)
    zero = jnp.zeros((RANK, COL), BF16)
    right = []
    for k in range(2):
        q1, q2 = pieces(q_total[RANK * k : RANK * (k + 1)], 2)
        for q in (q1, q2, q1):
            right.append(jnp.concatenate([q, zero] if k == 0 else [zero, q], axis=1))
    right = jnp.concatenate(right, axis=0)
    cot = jnp.concatenate([cot_ref[0], cot_ref[1]], axis=1)

    def left_of(columns):
        left = []
        for k in range(2):
            b1, b2 = pieces(basis_ref[RANK * k : RANK * (k + 1), columns], 2)
            left += [b1, b1, b2]
        return jnp.concatenate(left, axis=0)

    worker = worker_ref[0]
    first = pl.multiple_of((worker // 2) * 128, 128)
    tile_ref[...] = dot(left_of(pl.ds(first, 128)), right, TN_DIMS)
    mine = tile_ref[pl.ds(pl.multiple_of((worker % 2) * 64, 64), 64), :]
    approx_ref[0] = mine[:, :COL].astype(BF16)
    approx_ref[1] = mine[:, COL:].astype(BF16)

    minus = jnp.concatenate([cot, -right], axis=0)
    for t in range(NT):
        left = jnp.concatenate(
            [gathered_ref[:, GCOL * t : GCOL * t + BLK], left_of(slice(BLK * t, BLK * (t + 1)))], axis=0
        )
        value = dot(left, minus, TN_DIMS)
        for k in range(2):
            rows = slice(BLK * t, BLK * (t + 1))
            error = error_ref[k, rows, :].astype(F32)
            new_ref[k, rows, :] = (value[:, COL * k : COL * (k + 1)] + error).astype(BF16)


def input_kernel(core_ref, gathered_ref, weight_ref, keep_ref, send_ref):
    core = core_ref[0]
    for own in range(2):
        half = core if own else 1 - core
        total = jnp.zeros((TOK, BLK), F32)
        for x in range(NX):
            first = pl.multiple_of((NC * x + core) * GCOL + BLK, 128)
            cot = gathered_ref[:, pl.ds(first, 2 * COL)]
            weight = weight_ref[pl.ds(half * 8, 8), x].reshape(BLK, 2 * COL)
            total = total + dot(cot, weight, NT_DIMS)
        if own:
            keep_ref[...] = total
        else:
            send_ref[...] = total.astype(BF16)


def add_kernel(keep_ref, recv_ref, out_ref):
    out_ref[...] = (keep_ref[...] + recv_ref[...].astype(F32)).astype(BF16)


def exchange(value, axes):
    return lax.all_to_all(value, axes, 0, 0, tiled=True)


def shards(normed, kv_cotangent, kv_weight, error_buffer, q_factor):
    error = error_buffer[0]
    local = jnp.concatenate([normed, kv_cotangent[0], kv_cotangent[1]], axis=1)
    gathered = lax.all_gather(local, ("x", "core"), axis=1, tiled=True)

    sent = call(first_kernel, shape((NT, ROWS, BLK + TOKP)), error, kv_cotangent, q_factor)
    sent = call(second_kernel, shape((NY, 40, BLK)), exchange(sent, ("x", "core")), normed, kv_weight)
    sent, weight = call(
        third_kernel, (shape((NZ, 8, BLK)), shape((NY, 64, 2 * COL), BF16)), exchange(sent, ("y",))
    )
    weight = exchange(weight, ("x",))
    weight = lax.all_gather(weight, "z", axis=0, tiled=False)
    sent = call(
        lambda *refs: repeat_kernel(1.0 / WORKERS, *refs), shape((NY * NT, 8, BLK)), exchange(sent, ("z",))
    )
    recv = exchange(sent, ("y", "x", "core"))
    basis, term = call(
        basis_kernel,
        (shape((ROWS, D)), shape((NZ, ROWS, COL))),
        recv,
        gathered,
        kv_cotangent,
        error,
        scratch=[pltpu.VMEM((ROWS, D), F32), pltpu.VMEM((ROWS, D), F32)],
    )
    term = call(lambda *refs: repeat_kernel(1.0, *refs), shape((NY, ROWS, COL)), exchange(term, ("z",)))
    term = exchange(term, ("y",))
    worker = lax.axis_index(("y", "z")).astype(jnp.int32).reshape(1)
    approx, new_error = call(
        final_kernel,
        (shape((2, 64, COL), BF16), shape((2, D, COL), BF16)),
        worker,
        term,
        basis,
        gathered,
        kv_cotangent,
        error,
        scratch=[pltpu.VMEM((COL, 2 * COL), F32)],
        specs=[SMEM] + [VMEM] * 5,
    )
    core = lax.axis_index("core").astype(jnp.int32).reshape(1)
    approx, weight = lax.optimization_barrier((approx, weight))
    keep, give = call(
        input_kernel,
        (shape((TOK, BLK)), shape((TOK, BLK), BF16)),
        core,
        gathered,
        weight,
        specs=[SMEM, VMEM, VMEM],
    )
    take = lax.ppermute(give, "core", [(0, 1), (1, 0)])
    input_grad = call(add_kernel, shape((TOK, BLK), BF16), keep, take)
    return (input_grad, approx, new_error[None])


def solution(mesh):
    whole = Mesh(mesh.devices.reshape(NY, NZ, NX, NC), ("y", "z", "x", "core"))
    dp, tensor = ("y", "z"), ("x", "core")
    in_specs = (
        P(dp, tensor),
        P(None, dp, tensor),
        P(None, dp, tensor),
        P(dp, None, None, tensor),
        P(None, None, tensor),
    )
    out_specs = (P(dp, tensor), P(None, dp, tensor), P(dp, None, None, tensor))
    return jax.shard_map(shards, mesh=whole, in_specs=in_specs, out_specs=out_specs, check_vma=False)
```

time: 1010 us -> 168 us (0.17)
  the two profiles are of different devices: /device:TPU:2 before, /device:TPU:1 now
where the time goes in v1:
time: 168 us; the launch traced here: 167 us
  blocking collectives  110 us (65%)
  between operations  14.1 us (8%)
  Pallas kernels  12 us (7%)
  starting transfers between devices  11.5 us (7%)
  local copies, waits for them, and re-layouts  11.1 us (7%)
  waiting for transfers between devices  5.82 us (3%)
  other arithmetic  1.85 us (1%)
    all_to_all x6, blocking collectives, exchange(): return lax.all_to_all(value, axes, 0, 0, tiled=True)  110 us
    pallas_call x9, Pallas kernels, call(): pl.pallas_call(kernel, out_shape=out_shape, in_specs=specs or [VMEM] * le...  12 us
    unnamed x20, local copies, waits for them, and re-layouts  10.1 us
    ppermute x1, starting transfers between devices, shards(): take = lax.ppermute(give, 'core', [(0, 1), (1, 0)])  8.06 us
    all_to_all x1, waiting for transfers between devices, exchange(): return lax.all_to_all(value, axes, 0, 0, tiled=True)  4.48 us
  transfers between devices with their start and end apart: 4, of which 2 were waited for; matrix products, arithmetic and copies ran while one was open for 0% of the time, Pallas kernels for 6%

profile of v1, /device:TPU:1, one launch (start us, length us, event | category | flops | bytes accessed | tf_op | source)
XLA Modules:
  0.0 166.8 jit_solution(3432212154310500856)
XLA Ops:
  7.2 1.0 slice_bitcast_fusion.1
  8.2 1.8 %pad_maximum_fusion = bf16[368,768]{1,0:T(8,128)(2,1)} fusion(bf16[368,128]{1,0:T(8,128)(2,1)S(1)} %get-tuple-element.24, bf16[368,128]{1,0:T(8,128)(2,1)S(1)} %get-tuple-element.23, bf16[368,512]{1,0:T(8,128)(2,1)} %normed_ref.1), kind=kLoop, calls=%fused_computation | loop fusion | flops 1695744 | bytes 1130496 | tf_op jit(solution)/shard_map/concatenate | solution.py:204
  10.2 1.6 copy-done.3
  11.8 0.8 shard_map.76
  12.5 23.2 %all_to_all.35.recv_ref = f32[8,32,896]{2,1,0:T(8,128)S(1)} all-to-all(f32[8,32,896]{2,1,0:T(8,128)S(1)} %shard_map.76), channel_id=1, replica_groups=mesh['y'=4,'z'=16,'x'=4,'core'=2] {'x','core'}, dimensions={0} | all-to-all | bytes 1835008 | tf_op jit(solution)/shard_map/all_to_all | solution.py:199
  35.8 0.2 shard_map.77
  36.0 8.9 %all_to_all.36.recv_ref = f32[4,40,512]{2,1,0:T(8,128)S(1)} all-to-all(f32[4,40,512]{2,1,0:T(8,128)S(1)} %shard_map.77), channel_id=1, replica_groups=mesh['y'=4,'z'=16,'x'=4,'core'=2] {'y'}, dimensions={0} | all-to-all | bytes 655360 | tf_op jit(solution)/shard_map/all_to_all | solution.py:199
  44.9 9.2 %all_to_all.37 = bf16[4,64,256]{2,1,0:T(8,128)(2,1)} all-to-all(bf16[4,64,256]{2,1,0:T(8,128)(2,1)S(1)} %get-tuple-element.17), channel_id=1, replica_groups=mesh['y'=4,'z'=16,'x'=4,'core'=2] {'x'}, dimensions={0} | all-to-all | bytes 262144 | tf_op jit(solution)/shard_map/all_to_all | solution.py:199
  54.2 25.0 %all_to_all.38.refs_0_ = f32[16,8,512]{2,1,0:T(8,128)S(1)} all-to-all(f32[16,8,512]{2,1,0:T(8,128)S(1)} %get-tuple-element.13), channel_id=1, replica_groups=mesh['y'=4,'z'=16,'x'=4,'core'=2] {'z'}, dimensions={0} | all-to-all | bytes 524288 | tf_op jit(solution)/shard_map/all_to_all | solution.py:199
  79.3 22.1 %all_to_all.39.recv_ref = f32[32,8,512]{2,1,0:T(8,128)S(1)} all-to-all(f32[32,8,512]{2,1,0:T(8,128)S(1)} %shard_map.79), channel_id=1, replica_groups=mesh['y'=4,'z'=16,'x'=4,'core'=2] {'y','x','core'}, dimensions={0} | all-to-all | bytes 1048576 | tf_op jit(solution)/shard_map/all_to_all | solution.py:199
  101.4 2.3 %copy-done = bf16[368,6144]{1,0:T(8,128)(2,1)S(1)} copy-done((bf16[368,6144]{1,0:T(8,128)(2,1)S(1)}, bf16[368,6144]{1,0:T(8,128)(2,1)}, u32[]{:S(2)}) %copy-start) | copy-done | bytes 4522008
  103.7 5.7 %shard_map.80 = (f32[32,4096]{1,0:T(8,128)S(1)}, f32[16,32,128]{2,1,0:T(8,128)S(1)}) custom-call(f32[32,8,512]{2,1,0:T(8,128)S(1)} %all_to_all.39.recv_ref, bf16[368,6144]{1,0:T(8,128)(2,1)S(1)} %copy-done, bf16[2,368,128]{2,1,0:T(8,128)(2,1)S(1)} %copy-done.5, bf16[2,4096,128]{2,1,0:T(8,128)(2,1)S(1)} %bitcast.10), custom_call_target="tpu_custom_call" | custom-call | tf_op jit(solution)/shard_map/pallas_call | solution.py:45
  109.4 22.1 %all_to_all.40.refs_0_ = f32[16,32,128]{2,1,0:T(8,128)S(1)} all-to-all(f32[16,32,128]{2,1,0:T(8,128)S(1)} %get-tuple-element.14), channel_id=1, replica_groups=mesh['y'=4,'z'=16,'x'=4,'core'=2] {'z'}, dimensions={0} | all-to-all | bytes 524288 | tf_op jit(solution)/shard_map/all_to_all | solution.py:199
  131.5 0.7 shard_map.81
  132.1 3.3 %all-to-all-start.5 = ((f32[4,32,128]{2,1,0:T(8,128)}), f32[4,32,128]{2,1,0:T(8,128)S(1)}, u32[]{:S(2)}, u32[]{:S(2)}) async-start(f32[4,32,128]{2,1,0:T(8,128)} %shard_map.81), calls=%async_computation.5 | async-start | bytes 131072 | tf_op jit(solution)/shard_map/all_to_all | solution.py:199
  135.5 4.5 %all-to-all-done.5.recv_ref = f32[4,32,128]{2,1,0:T(8,128)S(1)} async-done(((f32[4,32,128]{2,1,0:T(8,128)}), f32[4,32,128]{2,1,0:T(8,128)S(1)}, u32[]{:S(2)}, u32[]{:S(2)}) %all-to-all-start.5) | async-done | bytes 65568 | tf_op jit(solution)/shard_map/all_to_all | solution.py:199
  139.9 2.3 %copy-done.1 = bf16[368,6144]{1,0:T(8,128)(2,1)S(1)} copy-done((bf16[368,6144]{1,0:T(8,128)(2,1)S(1)}, bf16[368,6144]{1,0:T(8,128)(2,1)}, u32[]{:S(2)}) %copy-start.1) | copy-done | bytes 4522008
  142.2 2.7 %shard_map.82 = (bf16[2,64,128]{2,1,0:T(8,128)(2,1)}, bf16[2,4096,128]{2,1,0:T(8,128)(2,1)}) custom-call(s32[1]{0:T(128)} %bitcast.3.worker_ref, f32[4,32,128]{2,1,0:T(8,128)S(1)} %all-to-all-done.5.recv_ref, f32[32,4096]{1,0:T(8,128)S(1)} %get-tuple-element.15.basis_ref, bf16[368,6144]{1,0:T(8,128)(2,1)S(1)} %copy-done.1, ...), custom_call_target="tpu_custom_call" | custom-call | tf_op jit(solution)/shard_map/pallas_call | solution.py:45
  144.9 2.3 %copy-done.2 = bf16[368,6144]{1,0:T(8,128)(2,1)S(1)} copy-done((bf16[368,6144]{1,0:T(8,128)(2,1)S(1)}, bf16[368,6144]{1,0:T(8,128)(2,1)}, u32[]{:S(2)}) %copy-start.2) | copy-done | bytes 4522008
  147.2 1.6 copy-done.6
  148.8 1.0 shard_map.83
  149.8 8.1 %collective-permute-start = (bf16[368,512]{1,0:T(8,128)(2,1)S(1)}, bf16[368,512]{1,0:T(8,128)(2,1)S(1)}, u32[]{:S(2)}, u32[]{:S(2)}) collective-permute-start(bf16[368,512]{1,0:T(8,128)(2,1)S(1)} %get-tuple-element.20), channel_id=1, source_target_pairs={{0,1},{1,0},{2,3},{3,2},{4,5},{5,4},{6,7},{7,6},{8,9},{9,8},{10,11... | collective-permute-start | bytes 1130504 | tf_op jit(solution)/shard_map/ppermute | solution.py:252
  157.9 1.3 collective-permute-done.recv_ref
  159.2 0.8 shard_map.84
  (23 shorter events, 0.2 us)
Async XLA Ops:
  7.2 3.0 %copy-start.5 = (bf16[2,368,128]{2,1,0:T(8,128)(2,1)S(1)}, bf16[2,368,128]{2,1,0:T(8,128)(2,1)}, u32[]{:S(2)}) copy-start(bf16[2,368,128]{2,1,0:T(8,128)(2,1)} %cot_ref.5) | copy-start | bytes 565252
  7.2 3.0 %copy-start.9 = (f32[2,16,128]{2,1,0:T(8,128)S(1)}, f32[2,16,128]{2,1,0:T(8,128)}, u32[]{:S(2)}) copy-start(f32[2,16,128]{2,1,0:T(8,128)} %q_ref.1) | copy-start | bytes 49156
  7.2 94.2 %all-gather.4.cloned.1.call-start = ((), (), s32[]{:S(2)}) async-start(), calls=%async_computation.7 | async-start | bytes 5087232 | tf_op jit(solution)/shard_map/all_gather | solution.py:205
  10.1 134.8 %all-gather.6.cloned.1.call-start = ((), (), s32[]{:S(2)}) async-start(), calls=%async_computation.8 | async-start | bytes 2228224 | tf_op jit(solution)/shard_map/all_gather | solution.py:213
  10.2 1.6 copy-start.3
  12.5 23.2 %copy-start.7 = (bf16[368,512]{1,0:T(8,128)(2,1)S(1)}, bf16[368,512]{1,0:T(8,128)(2,1)}, u32[]{:S(2)}) copy-start(bf16[368,512]{1,0:T(8,128)(2,1)} %normed_ref.1) | copy-start | bytes 1130500
  12.5 23.2 %copy-start.8 = (bf16[2,64,128]{2,1,0:T(8,128)(2,1)S(1)}, bf16[2,64,128]{2,1,0:T(8,128)(2,1)}, u32[]{:S(2)}) copy-start(bf16[2,64,128]{2,1,0:T(8,128)(2,1)} %weight_ref.1) | copy-start | bytes 98308
  54.2 47.2 %copy-start.4 = (bf16[1,2,4096,128]{3,2,1,0:T(8,128)(2,1)S(1)}, bf16[1,2,4096,128]{3,2,1,0:T(8,128)(2,1)}, u32[]{:S(2)}) copy-start(bf16[1,2,4096,128]{3,2,1,0:T(8,128)(2,1)} %param.8) | copy-start | bytes 6291460
  101.4 2.3 %copy-start = (bf16[368,6144]{1,0:T(8,128)(2,1)S(1)}, bf16[368,6144]{1,0:T(8,128)(2,1)}, u32[]{:S(2)}) copy-start(bf16[368,6144]{1,0:T(8,128)(2,1)} %all-gather.4.cloned.1.call-done.gathered_ref) | copy-start | bytes 13565956
  132.1 7.8 %all-to-all-start.5 = ((f32[4,32,128]{2,1,0:T(8,128)}), f32[4,32,128]{2,1,0:T(8,128)S(1)}, u32[]{:S(2)}, u32[]{:S(2)}) async-start(f32[4,32,128]{2,1,0:T(8,128)} %shard_map.81), calls=%async_computation.5 | async-start | bytes 131072 | tf_op jit(solution)/shard_map/all_to_all | solution.py:199
  139.9 2.3 %copy-start.1 = (bf16[368,6144]{1,0:T(8,128)(2,1)S(1)}, bf16[368,6144]{1,0:T(8,128)(2,1)}, u32[]{:S(2)}) copy-start(bf16[368,6144]{1,0:T(8,128)(2,1)} %all-gather.4.cloned.1.call-done.gathered_ref) | copy-start | bytes 13565956
  144.9 2.3 %copy-start.2 = (bf16[368,6144]{1,0:T(8,128)(2,1)S(1)}, bf16[368,6144]{1,0:T(8,128)(2,1)}, u32[]{:S(2)}) copy-start(bf16[368,6144]{1,0:T(8,128)(2,1)} %all-gather.4.cloned.1.call-done.gathered_ref) | copy-start | bytes 13565956
  147.2 1.6 copy-start.6
  149.8 9.4 %collective-permute-start = (bf16[368,512]{1,0:T(8,128)(2,1)S(1)}, bf16[368,512]{1,0:T(8,128)(2,1)S(1)}, u32[]{:S(2)}, u32[]{:S(2)}) collective-permute-start(bf16[368,512]{1,0:T(8,128)(2,1)S(1)} %get-tuple-element.20), channel_id=1, source_target_pairs={{0,1},{1,0},{2,3},{3,2},{4,5},{5,4},{6,7},{7,6},{8,9},{9,8},{10,11... | collective-permute-start | bytes 1130504 | tf_op jit(solution)/shard_map/ppermute | solution.py:252
Sparse Core Ops, SparseCore 0:
  10.7 48.2 all-gather.3
  61.1 73.2 all-gather.5

commit v2 on v1

v2 whole, which is shorter than its diff:
```python
import jax
import jax.numpy as jnp
from jax import lax
from jax.experimental import pallas as pl
from jax.experimental.pallas import tpu as pltpu
from jax.sharding import Mesh
from jax.sharding import PartitionSpec as P

EPSILON = 1e-06
WORKERS = 64
NY, NZ, NX, NC = 4, 16, 4, 2
NT = NX * NC
RANK = 16
ROWS = 2 * RANK
D = 4096
BLK = D // NT
TOK = 368
TOKP = 384
COL = 128
GCOL = BLK + 2 * COL
F32 = jnp.float32
BF16 = jnp.bfloat16
VMEM = pl.BlockSpec(memory_space=pltpu.VMEM)
SMEM = pl.BlockSpec(memory_space=pltpu.SMEM)
HBM = pl.BlockSpec(memory_space=pl.ANY)
NT_DIMS = (((1,), (1,)), ((), ()))
NN_DIMS = (((1,), (0,)), ((), ()))
TN_DIMS = (((0,), (0,)), ((), ()))


def dot(a, b, dims):
    return lax.dot_general(a, b, dims, preferred_element_type=F32)


def pieces(value, count):
    result = []
    for _ in range(count):
        part = value.astype(BF16)
        result.append(part)
        value = value - part.astype(F32)
    return result


def call(kernel, out_shape, *args, scratch=(), specs=None, outs=None, flops=0, moved=0):
    return pl.pallas_call(
        kernel,
        out_shape=out_shape,
        in_specs=specs or [VMEM] * len(args),
        out_specs=outs or jax.tree.map(lambda _: VMEM, out_shape),
        scratch_shapes=list(scratch),
        compiler_params=pltpu.CompilerParams(vmem_limit_bytes=24 * 2**20),
        cost_estimate=pl.CostEstimate(flops=flops, bytes_accessed=moved, transcendentals=0),
    )(*args)


def shape(dims, dtype=F32):
    return jax.ShapeDtypeStruct(dims, dtype)


def tall(value):
    return jnp.concatenate([value[:, 128 * j : 128 * (j + 1)] for j in range(value.shape[1] // 128)], axis=0)


def wide(value, rows):
    return jnp.concatenate([value[rows * j : rows * (j + 1)] for j in range(value.shape[0] // rows)], axis=1)


def added(ref, rows=slice(None)):
    total = ref[0, rows]
    for i in range(1, ref.shape[0]):
        total = total + ref[i, rows]
    return total


def block(t):
    return slice(BLK * t, BLK * (t + 1))


def first_kernel(error_hbm, normed_hbm, cot_hbm, cot_ref, q_ref, out_ref, error_ref, local_hbm, sems, local_sems):
    copies = [
        pltpu.make_async_copy(error_hbm.at[:, block(t), :], error_ref.at[:, block(t), :], sems.at[t])
        for t in range(NT)
    ]
    for copy in copies:
        copy.start()
    local = [pltpu.make_async_copy(normed_hbm, local_hbm.at[:, :BLK], local_sems.at[2])]
    for k in range(2):
        columns = slice(BLK + COL * k, BLK + COL * (k + 1))
        local.append(pltpu.make_async_copy(cot_hbm.at[k], local_hbm.at[:, columns], local_sems.at[k]))
    for copy in local:
        copy.start()
    q = [jnp.concatenate(pieces(q_ref[k], 3), axis=0) for k in range(2)]
    for k in range(2):
        token = dot(q[k], cot_ref[k], NT_DIMS)
        token = token[:RANK] + token[RANK : 2 * RANK] + token[2 * RANK :]
        token = jnp.concatenate([token, jnp.zeros((RANK, TOKP - TOK), F32)], axis=1)
        for t in range(NT):
            for j in range(3):
                first = ROWS * (4 + j) + RANK * k
                out_ref[t, first : first + RANK, :] = token[:, 128 * j : 128 * (j + 1)]
    for t in range(NT):
        copies[t].wait()
        for k in range(2):
            part = dot(q[k], error_ref[k, block(t), :], NT_DIMS)
            part = part[:RANK] + part[RANK : 2 * RANK] + part[2 * RANK :]
            for j in range(4):
                first = ROWS * j + RANK * k
                out_ref[t, first : first + RANK, :] = part[:, 128 * j : 128 * (j + 1)]
    for copy in local:
        copy.wait()


def second_kernel(recv_ref, normed_ref, out_ref):
    total = added(recv_ref)
    token = jnp.concatenate(pieces(wide(total[4 * ROWS :], ROWS)[:, :TOK], 3), axis=0)
    grad = dot(token, normed_ref[...], NN_DIMS)
    factor = wide(total[: 4 * ROWS], ROWS) + (grad[:ROWS] + grad[ROWS : 2 * ROWS] + grad[2 * ROWS :])
    for y in range(NY):
        out_ref[y] = tall(factor[8 * y : 8 * y + 8])


def third_kernel(recv_ref, weight_ref, out_ref):
    total = added(recv_ref)
    weight = [weight_ref[k].astype(F32) for k in range(2)]
    for z in range(NZ):
        out_ref[z, :32, :] = total
        for k in range(2):
            out_ref[z, 32 + 64 * k : 96 + 64 * k, :] = weight[k]


def fourth_kernel(recv_ref, out_ref, weight_ref):
    total = added(recv_ref, slice(0, 32)) * (1.0 / WORKERS)
    for i in range(NY * NT):
        out_ref[i] = total
    for z in range(NZ):
        weight_ref[z] = recv_ref[z, 32:, :].astype(BF16)


def basis_kernel(
    recv_ref, gathered_hbm, cot_ref, error_ref, basis_ref, term_ref, features_ref, p_ref, v_ref, sems
):
    copies = [
        pltpu.make_async_copy(
            gathered_hbm.at[:, GCOL * t : GCOL * t + BLK], features_ref.at[t], sems.at[t]
        )
        for t in range(NT)
    ]
    for copy in copies:
        copy.start()
    for y in range(NY):
        for t in range(NT):
            value = wide(recv_ref[NT * y + t], 8)
            p_ref[8 * y : 8 * y + 8, block(t)] = value
            v_ref[8 * y : 8 * y + 8, block(t)] = value
    for i in range(RANK):
        for k in range(2):
            row = RANK * k + i
            vector = v_ref[row : row + 1, :]
            square = jnp.sum(vector * vector, axis=1, keepdims=True) + EPSILON
            column = vector * (1.0 / jnp.sqrt(square))
            basis_ref[row : row + 1, :] = column
            if i < RANK - 1:
                rows = slice(RANK * k + 8 * ((i + 1) // 8), RANK * (k + 1))
                coeff = jnp.sum(p_ref[rows, :] * column, axis=1, keepdims=True)
                v_ref[rows, :] = v_ref[rows, :] - coeff * column
    basis = [
        jnp.concatenate(pieces(basis_ref[RANK * k : RANK * (k + 1), :], 3), axis=0) for k in range(2)
    ]
    both = jnp.concatenate(basis, axis=0)
    token = jnp.zeros((96, TOK), F32)
    for t in range(NT):
        copies[t].wait()
        token = token + dot(both[:, block(t)], features_ref[t], NT_DIMS)
    for k in range(2):
        part = token[48 * k : 48 * (k + 1)]
        part = part[:RANK] + part[RANK : 2 * RANK] + part[2 * RANK :]
        part = jnp.concatenate(pieces(part, 3), axis=0)
        term = dot(part, cot_ref[k], NN_DIMS) + dot(basis[k], error_ref[k], NN_DIMS)
        term = term[:RANK] + term[RANK : 2 * RANK] + term[2 * RANK :]
        for z in range(NZ):
            term_ref[z, RANK * k : RANK * (k + 1), :] = term


def repeat_kernel(recv_ref, out_ref):
    total = added(recv_ref)
    for i in range(out_ref.shape[0]):
        out_ref[i] = total


def final_kernel(
    worker_ref,
    recv_ref,
    basis_ref,
    features_ref,
    cot_ref,
    error_ref,
    approx_ref,
    new_hbm,
    tile_ref,
    new_ref,
    sems,
):
    q_total = added(recv_ref) * (1.0 / WORKERS)
    zero = jnp.zeros((RANK, COL), BF16)
    right = []
    for k in range(2):
        q1, q2 = pieces(q_total[RANK * k : RANK * (k + 1)], 2)
        for q in (q1, q2, q1):
            right.append(jnp.concatenate([q, zero] if k == 0 else [zero, q], axis=1))
    right = jnp.concatenate(right, axis=0)
    cot = jnp.concatenate([cot_ref[0], cot_ref[1]], axis=1)

    def left_of(columns):
        left = []
        for k in range(2):
            b1, b2 = pieces(basis_ref[RANK * k : RANK * (k + 1), columns], 2)
            left += [b1, b1, b2]
        return jnp.concatenate(left, axis=0)

    minus = jnp.concatenate([cot, -right], axis=0)
    copies = []
    for t in range(NT):
        left = jnp.concatenate([features_ref[t], left_of(block(t))], axis=0)
        value = dot(left, minus, TN_DIMS)
        for k in range(2):
            error = error_ref[k, block(t), :].astype(F32)
            new_ref[k, block(t), :] = (value[:, COL * k : COL * (k + 1)] + error).astype(BF16)
        copy = pltpu.make_async_copy(new_ref.at[:, block(t), :], new_hbm.at[:, block(t), :], sems.at[t])
        copy.start()
        copies.append(copy)

    worker = worker_ref[0]
    first = pl.multiple_of((worker // 2) * 128, 128)
    tile_ref[...] = dot(left_of(pl.ds(first, 128)), right, TN_DIMS)
    mine = tile_ref[pl.ds(pl.multiple_of((worker % 2) * 64, 64), 64), :]
    approx_ref[0] = mine[:, :COL].astype(BF16)
    approx_ref[1] = mine[:, COL:].astype(BF16)
    for copy in copies:
        copy.wait()


def half_product(core, half, gathered_hbm, weight_hbm, cot_ref, part_ref, sems):
    copies = []
    for x in range(NX):
        first = pl.multiple_of((NC * x + core) * GCOL + BLK, 128)
        copies.append(
            (
                pltpu.make_async_copy(gathered_hbm.at[:, pl.ds(first, 2 * COL)], cot_ref.at[x], sems.at[0, x]),
                pltpu.make_async_copy(weight_hbm.at[x, pl.ds(half * 8, 8)], part_ref.at[x], sems.at[1, x]),
            )
        )
    for one, other in copies:
        one.start()
        other.start()
    total = jnp.zeros((TOK, BLK), F32)
    for x in range(NX):
        for copy in copies[x]:
            copy.wait()
        weight = [part_ref[x, :, 64 * k : 64 * (k + 1), :].reshape(BLK, COL) for k in range(2)]
        total = total + dot(cot_ref[x], jnp.concatenate(weight, axis=1), NT_DIMS)
    return total


def give_kernel(core_ref, gathered_hbm, weight_hbm, out_ref, cot_ref, part_ref, sems):
    core = core_ref[0]
    out_ref[...] = half_product(core, 1 - core, gathered_hbm, weight_hbm, cot_ref, part_ref, sems).astype(BF16)


def keep_kernel(core_ref, gathered_hbm, weight_hbm, take_ref, out_ref, cot_ref, part_ref, sems):
    core = core_ref[0]
    total = half_product(core, core, gathered_hbm, weight_hbm, cot_ref, part_ref, sems)
    out_ref[...] = (total + take_ref[...].astype(F32)).astype(BF16)


def exchange(value, axes):
    return lax.all_to_all(value, axes, 0, 0, tiled=True)


def shards(normed, kv_cotangent, kv_weight, error_buffer, q_factor):
    dma = pltpu.SemaphoreType.DMA
    swap = [(NX * i + j, NX * j + i) for i in range(NY) for j in range(NX)]
    weight = lax.ppermute(kv_weight, ("y", "x"), swap)
    sent, error, local = call(
        first_kernel,
        (shape((NT, 7 * ROWS, 128)), shape((2, D, COL), BF16), shape((TOK, GCOL), BF16)),
        error_buffer[0],
        normed,
        kv_cotangent,
        kv_cotangent,
        q_factor,
        specs=[HBM, HBM, HBM, VMEM, VMEM],
        outs=(VMEM, VMEM, HBM),
        scratch=[dma((NT,)), dma((3,))],
    )
    recv = exchange(sent, ("x", "core"))
    recv, local = lax.optimization_barrier((recv, local))
    gathered = lax.all_gather(local, ("x", "core"), axis=1, tiled=True)
    recv = exchange(call(second_kernel, shape((NY, 32, 128)), recv, normed), ("y",))
    recv = exchange(call(third_kernel, shape((NZ, 160, 128)), recv, weight), ("z",))
    sent, weight = call(fourth_kernel, (shape((NY * NT, 32, 128)), shape((NZ, 128, 128), BF16)), recv)
    weight = lax.all_gather(weight, "y", axis=0, tiled=False)
    basis, term, features = call(
        basis_kernel,
        (shape((ROWS, D)), shape((NZ, ROWS, COL)), shape((NT, TOK, BLK), BF16)),
        exchange(sent, ("y", "x", "core")),
        gathered,
        kv_cotangent,
        error,
        specs=[VMEM, HBM, VMEM, VMEM],
        scratch=[pltpu.VMEM((ROWS, D), F32), pltpu.VMEM((ROWS, D), F32), dma((NT,))],
    )
    term = exchange(call(repeat_kernel, shape((NY, ROWS, COL)), exchange(term, ("z",))), ("y",))
    term, weight = lax.optimization_barrier((term, weight))
    core = lax.axis_index("core").astype(jnp.int32).reshape(1)
    product_scratch = [
        pltpu.VMEM((NX, TOK, 2 * COL), BF16),
        pltpu.VMEM((NX, 8, 128, COL), BF16),
        dma((2, NX)),
    ]
    give = call(
        give_kernel,
        shape((TOK, BLK), BF16),
        core,
        gathered,
        weight,
        specs=[SMEM, HBM, HBM],
        scratch=product_scratch,
    )
    take = lax.ppermute(give, "core", [(0, 1), (1, 0)])
    term, give = lax.optimization_barrier((term, give))
    worker = lax.axis_index(("y", "z")).astype(jnp.int32).reshape(1)
    approx, new_error = call(
        final_kernel,
        (shape((2, 64, COL), BF16), shape((2, D, COL), BF16)),
        worker,
        term,
        basis,
        features,
        kv_cotangent,
        error,
        specs=[SMEM] + [VMEM] * 5,
        outs=(VMEM, HBM),
        scratch=[pltpu.VMEM((COL, 2 * COL), F32), pltpu.VMEM((2, D, COL), BF16), dma((NT,))],
    )
    approx, take = lax.optimization_barrier((approx, take))
    input_grad = call(
        keep_kernel,
        shape((TOK, BLK), BF16),
        core,
        gathered,
        weight,
        take,
        specs=[SMEM, HBM, HBM, VMEM],
        scratch=product_scratch,
    )
    return (input_grad, approx, new_error[None])


def solution(mesh):
    whole = Mesh(mesh.devices.reshape(NY, NZ, NX, NC), ("y", "z", "x", "core"))
    dp, tensor = ("y", "z"), ("x", "core")
    in_specs = (
        P(dp, tensor),
        P(None, dp, tensor),
        P(None, dp, tensor),
        P(dp, None, None, tensor),
        P(None, None, tensor),
    )
    out_specs = (P(dp, tensor), P(None, dp, tensor), P(dp, None, None, tensor))
    return jax.shard_map(shards, mesh=whole, in_specs=in_specs, out_specs=out_specs, check_vma=False)
```

time: 168 us -> 213 us (1.27)
  blocking collectives: 110 us -> 139 us
  Pallas kernels: 12 us -> 17.9 us
  local copies, waits for them, and re-layouts: 11.1 us -> 16.9 us
  starting transfers between devices: 11.5 us -> 15.7 us
  waiting for transfers between devices: 5.82 us -> 8.22 us
    all_to_all x6 -> x4, blocking collectives: 110 us -> 139 us  [exchange(): return lax.all_to_all(value, axes, 0, 0, tiled=True)]
    unnamed x20 -> x30, local copies, waits for them, and re-layouts: 10.1 us -> 16.9 us
    pallas_call x9, Pallas kernels: 12 us -> 17.9 us  [call(): pl.pallas_call(kernel, out_shape=out_shape, in_specs=specs or [VMEM] * le...]
    all_to_all x1 -> x2, starting transfers between devices: 3.32 us -> 7.52 us  [exchange(): return lax.all_to_all(value, axes, 0, 0, tiled=True)]
    all_to_all x1 -> x2, waiting for transfers between devices: 4.48 us -> 8.17 us  [exchange(): return lax.all_to_all(value, axes, 0, 0, tiled=True)]
  transfers between devices with their start and end apart: 4 -> 6, of which waited for: 2 -> 2; matrix products, arithmetic and copies ran while one was open for 0% -> 0% of each run, Pallas kernels for 6% -> 6%
where the time goes in v2:
time: 213 us; the launch traced here: 212 us
  blocking collectives  139 us (65%)
  Pallas kernels  17.9 us (8%)
  local copies, waits for them, and re-layouts  16.9 us (8%)
  starting transfers between devices  15.7 us (7%)
  between operations  14.2 us (7%)
  waiting for transfers between devices  8.22 us (4%)
    all_to_all x4, blocking collectives, exchange(): return lax.all_to_all(value, axes, 0, 0, tiled=True)  139 us
    pallas_call x9, Pallas kernels, call(): pl.pallas_call(kernel, out_shape=out_shape, in_specs=specs or [VMEM] * le...  17.9 us
    unnamed x30, local copies, waits for them, and re-layouts  16.9 us
    all_to_all x2, waiting for transfers between devices, exchange(): return lax.all_to_all(value, axes, 0, 0, tiled=True)  8.17 us
    all_to_all x2, starting transfers between devices, exchange(): return lax.all_to_all(value, axes, 0, 0, tiled=True)  7.52 us
    ppermute x1, starting transfers between devices, shards(): take = lax.ppermute(give, 'core', [(0, 1), (1, 0)])  7.41 us
  transfers between devices with their start and end apart: 6, of which 2 were waited for; matrix products, arithmetic and copies ran while one was open for 0% of the time, Pallas kernels for 6%

profile of v2, /device:TPU:1, one launch (start us, length us, event | category | flops | bytes accessed | tf_op | source)
XLA Modules:
  0.0 211.9 jit_solution(884447606658078457)
XLA Ops:
  7.2 0.9 copy-done.7
  8.1 1.6 copy-done.9
  9.7 1.0 copy-done.10
  11.4 2.2 %shard_map.76 = (f32[8,224,128]{2,1,0:T(8,128)S(1)}, bf16[2,4096,128]{2,1,0:T(8,128)(2,1)S(1)}, bf16[368,768]{1,0:T(8,128)(2,1)S(1)}) custom-call(bf16[2,4096,128]{2,1,0:T(8,128)(2,1)S(1)} %bitcast.7, bf16[368,512]{1,0:T(8,128)(2,1)S(1)} %copy-done.10, bf16[2,368,128]{2,1,0:T(8,128)(2,1)S(1)} %copy-done.7, bf16[2,368,128]{2,1,0:T(8,128)(2,1)S(1)} %copy-done.7, ...), custom_call_target="tpu_custom_call" | custom-call | tf_op jit(solution)/shard_map/pallas_call | solution.py:45
  14.4 23.2 %all_to_all.30.recv_ref = f32[8,224,128]{2,1,0:T(8,128)S(1)} all-to-all(f32[8,224,128]{2,1,0:T(8,128)S(1)} %get-tuple-element.20), channel_id=1, replica_groups=mesh['y'=4,'z'=16,'x'=4,'core'=2] {'x','core'}, dimensions={0} | all-to-all | bytes 1835008 | tf_op jit(solution)/shard_map/all_to_all | solution.py:276
  38.5 3.3 %all-to-all-start.1 = ((f32[4,32,128]{2,1,0:T(8,128)}), f32[4,32,128]{2,1,0:T(8,128)S(1)}, u32[]{:S(2)}, u32[]{:S(2)}) async-start(f32[4,32,128]{2,1,0:T(8,128)} %shard_map.77), calls=%async_computation.1 | async-start | bytes 131072 | tf_op jit(solution)/shard_map/all_to_all | solution.py:276
  42.5 3.7 %all-to-all-done.1.recv_ref = f32[4,32,128]{2,1,0:T(8,128)S(1)} async-done(((f32[4,32,128]{2,1,0:T(8,128)}), f32[4,32,128]{2,1,0:T(8,128)S(1)}, u32[]{:S(2)}, u32[]{:S(2)}) %all-to-all-start.1) | async-done | bytes 65568 | tf_op jit(solution)/shard_map/all_to_all | solution.py:276
  46.4 69.4 %all_to_all.31.recv_ref = f32[16,160,128]{2,1,0:T(8,128)S(1)} all-to-all(f32[16,160,128]{2,1,0:T(8,128)S(1)} %shard_map.78), channel_id=1, replica_groups=mesh['y'=4,'z'=16,'x'=4,'core'=2] {'z'}, dimensions={0} | all-to-all | bytes 2621440 | tf_op jit(solution)/shard_map/all_to_all | solution.py:276
  115.8 0.9 shard_map.79
  116.6 26.7 %all_to_all.32.recv_ref = f32[32,32,128]{2,1,0:T(8,128)S(1)} all-to-all(f32[32,32,128]{2,1,0:T(8,128)S(1)} %get-tuple-element.24), channel_id=1, replica_groups=mesh['y'=4,'z'=16,'x'=4,'core'=2] {'y','x','core'}, dimensions={0} | all-to-all | bytes 1048576 | tf_op jit(solution)/shard_map/all_to_all | solution.py:276
  143.4 2.3 %copy-done = bf16[368,6144]{1,0:T(8,128)(2,1)S(1)} copy-done((bf16[368,6144]{1,0:T(8,128)(2,1)S(1)}, bf16[368,6144]{1,0:T(8,128)(2,1)}, u32[]{:S(2)}) %copy-start) | copy-done | bytes 4522008
  145.7 6.6 %shard_map.80 = (f32[32,4096]{1,0:T(8,128)S(1)}, f32[16,32,128]{2,1,0:T(8,128)S(1)}, bf16[8,368,512]{2,1,0:T(8,128)(2,1)S(1)}) custom-call(f32[32,32,128]{2,1,0:T(8,128)S(1)} %all_to_all.32.recv_ref, bf16[368,6144]{1,0:T(8,128)(2,1)S(1)} %copy-done, bf16[2,368,128]{2,1,0:T(8,128)(2,1)S(1)} %copy-done.8, bf16[2,4096,128]{2,1,0:T(8,128)(2,1)S(1)} %get-tuple-element.25.error_ref), custom_call_target="tpu_custom_call" | custom-call | tf_op jit(solution)/shard_map/pallas_call | solution.py:45
  152.3 1.6 copy-done.5
  153.9 19.6 %all_to_all.33.recv_ref = f32[16,32,128]{2,1,0:T(8,128)S(1)} all-to-all(f32[16,32,128]{2,1,0:T(8,128)S(1)} %get-tuple-element.26), channel_id=1, replica_groups=mesh['y'=4,'z'=16,'x'=4,'core'=2] {'z'}, dimensions={0} | all-to-all | bytes 524288 | tf_op jit(solution)/shard_map/all_to_all | solution.py:276
  174.1 4.2 %all-to-all-start.5 = ((f32[4,32,128]{2,1,0:T(8,128)}), f32[4,32,128]{2,1,0:T(8,128)S(1)}, u32[]{:S(2)}, u32[]{:S(2)}) async-start(f32[4,32,128]{2,1,0:T(8,128)} %shard_map.81), calls=%async_computation.5 | async-start | bytes 131072 | tf_op jit(solution)/shard_map/all_to_all | solution.py:276
  178.4 4.5 %all-to-all-done.5.recv_ref = f32[4,32,128]{2,1,0:T(8,128)S(1)} async-done(((f32[4,32,128]{2,1,0:T(8,128)}), f32[4,32,128]{2,1,0:T(8,128)S(1)}, u32[]{:S(2)}, u32[]{:S(2)}) %all-to-all-start.5) | async-done | bytes 65568 | tf_op jit(solution)/shard_map/all_to_all | solution.py:276
  182.9 2.3 %copy-done.1 = bf16[368,6144]{1,0:T(8,128)(2,1)S(1)} copy-done((bf16[368,6144]{1,0:T(8,128)(2,1)S(1)}, bf16[368,6144]{1,0:T(8,128)(2,1)}, u32[]{:S(2)}) %copy-start.1) | copy-done | bytes 4522008
  185.1 1.6 copy-done.3
  186.7 1.0 shard_map.82
  187.8 7.4 %collective-permute-start.1 = (bf16[368,512]{1,0:T(8,128)(2,1)S(1)}, bf16[368,512]{1,0:T(8,128)(2,1)}, u32[]{:S(2)}, u32[]{:S(2)}) collective-permute-start(bf16[368,512]{1,0:T(8,128)(2,1)S(1)} %shard_map.82), channel_id=1, source_target_pairs={{0,1},{1,0},{2,3},{3,2},{4,5},{5,4},{6,7},{7,6},{8,9},{9,8},{10,11... | collective-permute-start | bytes 1130504 | tf_op jit(solution)/shard_map/ppermute | solution.py:329
  195.2 1.8 copy-done.6
  197.0 2.9 %shard_map.83 = (bf16[2,64,128]{2,1,0:T(8,128)(2,1)}, bf16[2,4096,128]{2,1,0:T(8,128)(2,1)}) custom-call(s32[1]{0:T(128)} %bitcast.3.worker_ref, f32[4,32,128]{2,1,0:T(8,128)S(1)} %all-to-all-done.5.recv_ref, f32[32,4096]{1,0:T(8,128)S(1)} %get-tuple-element.31.basis_ref, bf16[8,368,512]{2,1,0:T(8,128)(2,1)S(1)} %copy-done.6, ...), custom_call_target="tpu_custom_call" | custom-call | tf_op jit(solution)/shard_map/pallas_call | solution.py:45
  200.0 2.3 %copy-done.2 = bf16[368,6144]{1,0:T(8,128)(2,1)S(1)} copy-done((bf16[368,6144]{1,0:T(8,128)(2,1)S(1)}, bf16[368,6144]{1,0:T(8,128)(2,1)}, u32[]{:S(2)}) %copy-start.2) | copy-done | bytes 4522008
  202.2 2.8 %shard_map.84 = bf16[368,512]{1,0:T(8,128)(2,1)} custom-call(s32[1]{0:T(128)} %bitcast.core_ref, bf16[368,6144]{1,0:T(8,128)(2,1)S(1)} %copy-done.2, bf16[4,16,128,128]{3,2,1,0:T(8,128)(2,1)S(1)} %bitcast.6, bf16[368,512]{1,0:T(8,128)(2,1)} %collective-permute-done.1.take_ref), custom_call_target="tpu_custom_call" | custom-call | tf_op jit(solution)/shard_map/pallas_call | solution.py:45
  (33 shorter events, 4.0 us)
Async XLA Ops:
  7.2 136.2 %all-gather.4.cloned.1.call-start = ((), (), s32[]{:S(2)}) async-start(), calls=%async_computation.6 | async-start | bytes 5087232 | tf_op jit(solution)/shard_map/all_gather | solution.py:297
  7.2 0.9 copy-start.7
  8.1 1.6 copy-start.9
  9.7 1.0 copy-start.10
  10.7 0.7 copy-start.13
  11.4 26.2 %copy-start.11 = (bf16[368,512]{1,0:T(8,128)(2,1)S(1)}, bf16[368,512]{1,0:T(8,128)(2,1)}, u32[]{:S(2)}) copy-start(bf16[368,512]{1,0:T(8,128)(2,1)} %normed_ref.1) | copy-start | bytes 1130500
  13.6 0.8 copy-start.12
  14.4 27.4 %copy-start.14 = (bf16[2,64,128]{2,1,0:T(8,128)(2,1)S(1)}, bf16[2,64,128]{2,1,0:T(8,128)(2,1)}, u32[]{:S(2)}) copy-start(bf16[2,64,128]{2,1,0:T(8,128)(2,1)} %param.7) | copy-start | bytes 98308
  38.5 7.7 %all-to-all-start.1 = ((f32[4,32,128]{2,1,0:T(8,128)}), f32[4,32,128]{2,1,0:T(8,128)S(1)}, u32[]{:S(2)}, u32[]{:S(2)}) async-start(f32[4,32,128]{2,1,0:T(8,128)} %shard_map.77), calls=%async_computation.1 | async-start | bytes 131072 | tf_op jit(solution)/shard_map/all_to_all | solution.py:276
  41.8 136.6 %all-gather.6.cloned.1.call-start = ((), (), s32[]{:S(2)}) async-start(), calls=%async_computation.7 | async-start | bytes 2621440 | tf_op jit(solution)/shard_map/all_gather | solution.py:301
  41.8 0.7 collective-permute-start
  115.8 27.6 %copy-start.8 = (bf16[2,368,128]{2,1,0:T(8,128)(2,1)S(1)}, bf16[2,368,128]{2,1,0:T(8,128)(2,1)}, u32[]{:S(2)}) copy-start(bf16[2,368,128]{2,1,0:T(8,128)(2,1)} %cot_ref.5) | copy-start | bytes 565252
  143.4 2.3 %copy-start = (bf16[368,6144]{1,0:T(8,128)(2,1)S(1)}, bf16[368,6144]{1,0:T(8,128)(2,1)}, u32[]{:S(2)}) copy-start(bf16[368,6144]{1,0:T(8,128)(2,1)} %all-gather.4.cloned.1.call-done.gathered_hbm) | copy-start | bytes 13565956
  152.3 1.6 copy-start.5
  174.1 8.7 %all-to-all-start.5 = ((f32[4,32,128]{2,1,0:T(8,128)}), f32[4,32,128]{2,1,0:T(8,128)S(1)}, u32[]{:S(2)}, u32[]{:S(2)}) async-start(f32[4,32,128]{2,1,0:T(8,128)} %shard_map.81), calls=%async_computation.5 | async-start | bytes 131072 | tf_op jit(solution)/shard_map/all_to_all | solution.py:276
  182.9 2.3 %copy-start.1 = (bf16[368,6144]{1,0:T(8,128)(2,1)S(1)}, bf16[368,6144]{1,0:T(8,128)(2,1)}, u32[]{:S(2)}) copy-start(bf16[368,6144]{1,0:T(8,128)(2,1)} %all-gather.4.cloned.1.call-done.gathered_hbm) | copy-start | bytes 13565956
  185.1 1.6 copy-start.3
  187.8 12.2 %collective-permute-start.1 = (bf16[368,512]{1,0:T(8,128)(2,1)S(1)}, bf16[368,512]{1,0:T(8,128)(2,1)}, u32[]{:S(2)}, u32[]{:S(2)}) collective-permute-start(bf16[368,512]{1,0:T(8,128)(2,1)S(1)} %shard_map.82), channel_id=1, source_target_pairs={{0,1},{1,0},{2,3},{3,2},{4,5},{5,4},{6,7},{7,6},{8,9},{9,8},{10,11... | collective-permute-start | bytes 1130504 | tf_op jit(solution)/shard_map/ppermute | solution.py:329
  195.2 1.9 copy-start.6
  197.0 2.9 %copy-start.4 = (bf16[64,128,128]{2,1,0:T(8,128)(2,1)S(1)}, bf16[64,128,128]{2,1,0:T(8,128)(2,1)}, u32[]{:S(2)}) copy-start(bf16[64,128,128]{2,1,0:T(8,128)(2,1)} %all-gather.6.cloned.1.call-done) | copy-start | bytes 6291460
  200.0 2.3 %copy-start.2 = (bf16[368,6144]{1,0:T(8,128)(2,1)S(1)}, bf16[368,6144]{1,0:T(8,128)(2,1)}, u32[]{:S(2)}) copy-start(bf16[368,6144]{1,0:T(8,128)(2,1)} %all-gather.4.cloned.1.call-done.gathered_hbm) | copy-start | bytes 13565956
Sparse Core Ops, SparseCore 0:
  37.8 40.6 all-gather.3
  116.8 42.9 all-gather.5

commit v3 on v1

v3 whole, which is shorter than its diff:
```python
import functools

import jax
import jax.numpy as jnp
from jax import lax
from jax.experimental import pallas as pl
from jax.experimental.pallas import tpu as pltpu
from jax.sharding import Mesh
from jax.sharding import PartitionSpec as P

EPSILON = 1e-06
WORKERS = 64
NY, NH, NL, NX, NC = 4, 8, 2, 4, 2
NT = NX * NC
NM = NY * NL
NZ = NH * NL
BIG = 59 * 2**20
RANK = 16
ROWS = 2 * RANK
D = 4096
BLK = D // NT
TOK = 368
TOKP = 384
COL = 128
GCOL = BLK + 2 * COL
F32 = jnp.float32
BF16 = jnp.bfloat16
VMEM = pl.BlockSpec(memory_space=pltpu.VMEM)
SMEM = pl.BlockSpec(memory_space=pltpu.SMEM)
HBM = pl.BlockSpec(memory_space=pltpu.HBM)
NT_DIMS = (((1,), (1,)), ((), ()))
NN_DIMS = (((1,), (0,)), ((), ()))
TN_DIMS = (((0,), (0,)), ((), ()))


def dot(a, b, dims):
    return lax.dot_general(a, b, dims, preferred_element_type=F32)


def pieces(value, count):
    result = []
    for _ in range(count):
        part = value.astype(BF16)
        result.append(part)
        value = value - part.astype(F32)
    return result


def call(kernel, out_shape, *args, scratch=(), specs=None, outs=None, cost=None, limit=16 * 2**20):
    return pl.pallas_call(
        kernel,
        out_shape=out_shape,
        in_specs=specs or [VMEM] * len(args),
        out_specs=outs or jax.tree.map(lambda _: VMEM, out_shape),
        scratch_shapes=list(scratch),
        cost_estimate=cost and pl.CostEstimate(flops=cost[0], bytes_accessed=cost[1], transcendentals=0),
        compiler_params=pltpu.CompilerParams(vmem_limit_bytes=limit),
    )(*args)


def shape(dims, dtype=F32):
    return jax.ShapeDtypeStruct(dims, dtype)


def tall(value):
    return jnp.concatenate([value[:, 128 * j : 128 * (j + 1)] for j in range(value.shape[1] // 128)], axis=0)


def wide(value, rows):
    return jnp.concatenate([value[rows * j : rows * (j + 1)] for j in range(value.shape[0] // rows)], axis=1)


def added(ref, rows=slice(None)):
    total = ref[0, rows].astype(F32)
    for i in range(1, ref.shape[0]):
        total = total + ref[i, rows].astype(F32)
    return total


def block(t):
    return slice(BLK * t, BLK * (t + 1))


def started(copies):
    for copy in copies:
        copy.start()
    return copies


def first_kernel(
    error_hbm, normed_hbm, cot_hbm, q_hbm, out_ref, local_ref, q_ref, cot_ref, normed_ref, error_ref, sems
):
    q_copy, cot_copy, normed_copy = started(
        [
            pltpu.make_async_copy(q_hbm, q_ref, sems.at[0]),
            pltpu.make_async_copy(cot_hbm, cot_ref, sems.at[1]),
            pltpu.make_async_copy(normed_hbm, normed_ref, sems.at[2]),
        ]
    )
    loads = started([pltpu.make_async_copy(error_hbm.at[k], error_ref.at[k], sems.at[3 + k]) for k in range(2)])
    q_copy.wait()
    q = [jnp.concatenate(pieces(q_ref[k], 3), axis=0) for k in range(2)]
    cot_copy.wait()
    for k in range(2):
        local_ref[4 + k] = cot_ref[k]
        token = dot(q[k], cot_ref[k], NT_DIMS)
        token = token[:RANK] + token[RANK : 2 * RANK] + token[2 * RANK :]
        token = jnp.concatenate([token, jnp.zeros((RANK, TOKP - TOK), F32)], axis=1)
        for t in range(NT):
            for j in range(3):
                first = ROWS * (4 + j) + RANK * k
                out_ref[t, first : first + RANK, :] = token[:, 128 * j : 128 * (j + 1)]
    normed_copy.wait()
    for j in range(4):
        local_ref[j] = normed_ref[:, 128 * j : 128 * (j + 1)]
    for k in range(2):
        loads[k].wait()
        for t in range(NT):
            part = dot(q[k], error_ref[k, block(t), :], NT_DIMS)
            part = part[:RANK] + part[RANK : 2 * RANK] + part[2 * RANK :]
            for j in range(4):
                first = ROWS * j + RANK * k
                out_ref[t, first : first + RANK, :] = part[:, 128 * j : 128 * (j + 1)]


def second_kernel(recv_ref, normed_ref, weight_ref, out_ref):
    total = added(recv_ref)
    token = jnp.concatenate(pieces(wide(total[4 * ROWS :], ROWS)[:, :TOK], 3), axis=0)
    grad = dot(token, normed_ref[...], NN_DIMS)
    factor = wide(total[: 4 * ROWS], ROWS) + (grad[:ROWS] + grad[ROWS : 2 * ROWS] + grad[2 * ROWS :])
    weight = [weight_ref[k].astype(F32) for k in range(2)]
    for m in range(NM):
        y = m // NL
        out_ref[m, :32, :] = tall(factor[8 * y : 8 * y + 8])
        for k in range(2):
            out_ref[m, 32 + 64 * k : 96 + 64 * k, :] = weight[k]


def third_kernel(recv_ref, out_ref, weight_ref):
    total = added(recv_ref, slice(0, 32))
    for z in range(NH):
        out_ref[z] = total
    for m in range(NM):
        weight_ref[m] = recv_ref[m, 32:, :].astype(BF16)


def repeat_kernel(scale, recv_ref, after_ref, out_ref):
    total = added(recv_ref)
    if scale != 1.0:
        total = total * scale
    total = total.astype(out_ref.dtype)
    for i in range(out_ref.shape[0]):
        out_ref[i] = total


def features(gathered_ref, t):
    return jnp.concatenate([gathered_ref[t, j] for j in range(4)], axis=1)


def basis_kernel(recv_ref, basis_ref, p_ref, v_ref):
    for y in range(NY):
        rows = slice(8 * (y % 2), 8 * (y % 2) + 8)
        for t in range(NT):
            value = wide(recv_ref[NT * y + t], 8)
            p_ref[y // 2, rows, block(t)] = value
            v_ref[y // 2, rows, block(t)] = value
    for i in range(RANK):
        vector = v_ref[:, i : i + 1, :]
        square = jnp.sum(vector * vector, axis=2, keepdims=True) + EPSILON
        if i < RANK - 1:
            rows = slice(8 * ((i + 1) // 8), RANK)
            coeff = jnp.sum(p_ref[:, rows, :] * vector, axis=2, keepdims=True)
        inverse = 1.0 / jnp.sqrt(square)
        column = vector * inverse
        basis_ref[:, i : i + 1, :] = column
        if i < RANK - 1:
            v_ref[:, rows, :] = v_ref[:, rows, :] - (coeff * inverse) * column


def term_kernel(basis_ref, gathered_ref, cot_ref, error_ref, term_ref):
    basis = [jnp.concatenate(pieces(basis_ref[k], 3), axis=0) for k in range(2)]
    both = jnp.concatenate(basis, axis=0)
    token = jnp.zeros((96, TOK), F32)
    for t in range(NT):
        token = token + dot(both[:, block(t)], features(gathered_ref, t), NT_DIMS)
    for k in range(2):
        part = token[48 * k : 48 * (k + 1)]
        part = part[:RANK] + part[RANK : 2 * RANK] + part[2 * RANK :]
        part = jnp.concatenate(pieces(part, 3), axis=0)
        term = dot(part, cot_ref[k], NN_DIMS) + dot(basis[k], error_ref[k], NN_DIMS)
        term = (term[:RANK] + term[RANK : 2 * RANK] + term[2 * RANK :]).astype(BF16)
        for z in range(NZ):
            term_ref[z, RANK * k : RANK * (k + 1), :] = term


def ready_kernel(gathered_hbm, flag_ref):
    flag_ref[...] = jnp.zeros((8, 128), F32)


def moment_kernel(core_ref, gathered_ref, cot_ref, error_ref, after_ref, moment_ref, mine_ref, flag_ref):
    flag_ref[...] = jnp.zeros((8, 128), F32)
    cot = jnp.concatenate([cot_ref[0], cot_ref[1]], axis=1)
    for t in range(NT):
        value = dot(features(gathered_ref, t), cot, TN_DIMS)
        for k in range(2):
            error = error_ref[k, block(t), :].astype(F32)
            moment_ref[k, block(t), :] = value[:, COL * k : COL * (k + 1)] + error
    core = core_ref[0]
    for x in range(NX):
        mine_ref[x] = jnp.concatenate([gathered_ref[NC * x + core, 4], gathered_ref[NC * x + core, 5]], axis=1)


def final_kernel(worker_ref, recv_ref, basis_ref, moment_ref, approx_ref, new_hbm, flag_ref, tile_ref, new_ref, sems):
    flag_ref[...] = jnp.zeros((8, 128), F32)
    parts = [pl.ds(D // 2 * i, D // 2) for i in range(2)]
    q_total = added(recv_ref) * (1.0 / WORKERS)
    zero = jnp.zeros((RANK, COL), BF16)
    right = []
    for k in range(2):
        q1, q2 = pieces(q_total[RANK * k : RANK * (k + 1)], 2)
        for q in (q1, q2, q1):
            right.append(jnp.concatenate([q, zero] if k == 0 else [zero, q], axis=1))
    right = jnp.concatenate(right, axis=0)

    def left_of(columns):
        left = []
        for k in range(2):
            b1, b2 = pieces(basis_ref[k, :, columns], 2)
            left += [b1, b1, b2]
        return jnp.concatenate(left, axis=0)

    worker = worker_ref[0]
    first = pl.multiple_of((worker // 2) * 128, 128)
    tile_ref[...] = dot(left_of(pl.ds(first, 128)), right, TN_DIMS)
    rows = tile_ref[pl.ds(pl.multiple_of((worker % 2) * 64, 64), 64), :]
    approx_ref[0] = rows[:, :COL].astype(BF16)
    approx_ref[1] = rows[:, COL:].astype(BF16)
    stores = []
    for t in range(NT):
        value = dot(left_of(block(t)), right, TN_DIMS)
        for k in range(2):
            part = moment_ref[k, block(t), :] - value[:, COL * k : COL * (k + 1)]
            new_ref[k, block(t), :] = part.astype(BF16)
        if t % 4 == 3:
            done = parts[t // 4]
            stores += started(
                [pltpu.make_async_copy(new_ref.at[:, done, :], new_hbm.at[:, done, :], sems.at[t // 4])]
            )
    for copy in stores:
        copy.wait()


def product_kernel(core_ref, cot_ref, weight_ref, after_ref, keep_ref, give_ref):
    core = core_ref[0]
    for half in range(2):
        first = 4 * (core if half else 1 - core)
        total = jnp.zeros((TOK, BLK), F32)
        for x in range(NX):
            weight = [
                weight_ref[pl.ds(first, 4), NL * x : NL * (x + 1), 64 * k : 64 * (k + 1), :].reshape(BLK, COL)
                for k in range(2)
            ]
            total = total + dot(cot_ref[x], jnp.concatenate(weight, axis=1), NT_DIMS)
        if half:
            keep_ref[...] = total
        else:
            give_ref[...] = total.astype(BF16)


def add_kernel(keep_ref, take_ref, out_ref):
    out_ref[...] = (keep_ref[...] + take_ref[...].astype(F32)).astype(BF16)


def exchange(value, axes):
    return lax.all_to_all(value, axes, 0, 0, tiled=True)


def shards(normed, kv_cotangent, kv_weight, error_buffer, q_factor):
    dma = pltpu.SemaphoreType.DMA
    error = error_buffer[0]
    core = lax.axis_index("core").astype(jnp.int32).reshape(1)
    worker = lax.axis_index(("y", "zh", "zl")).astype(jnp.int32).reshape(1)
    q_factor, core, worker = lax.optimization_barrier((q_factor, core, worker))

    swap = [(NX * i + j, NX * j + i) for i in range(NY) for j in range(NX)]
    weight = lax.ppermute(kv_weight, ("y", "x"), swap)
    flag = shape((8, 128))
    sent, local = call(
        first_kernel,
        (shape((NT, 7 * ROWS, 128)), shape((6, TOK, 128), BF16)),
        error,
        normed,
        kv_cotangent,
        q_factor,
        specs=[HBM] * 4,
        scratch=[
            pltpu.VMEM((2, RANK, COL), F32),
            pltpu.VMEM((2, TOK, COL), BF16),
            pltpu.VMEM((TOK, BLK), BF16),
            pltpu.VMEM((2, D, COL), BF16),
            dma((5,)),
        ],
        limit=BIG,
    )
    gathered = lax.all_gather(local, ("x", "core"), axis=0, tiled=False)
    ready = call(ready_kernel, flag, gathered, specs=[HBM], limit=BIG)
    other_core = [(0, 1), (1, 0)]
    recv = exchange(sent, ("x", "core"))
    recv = exchange(call(second_kernel, shape((NM, 160, 128)), recv, normed, weight), ("y", "zl"))
    sent, weight = call(third_kernel, (shape((NH, 32, 128)), shape((NM, 128, 128), BF16)), recv)
    weight = lax.all_gather(weight, "zh", axis=0, tiled=False)
    mean = functools.partial(repeat_kernel, 1.0 / WORKERS)
    sent = call(mean, shape((NY * NT, 32, 128)), exchange(sent, ("zh",)), ready)
    basis = call(
        basis_kernel,
        shape((2, RANK, D)),
        exchange(sent, ("y", "x", "core")),
        scratch=[pltpu.VMEM((2, RANK, D), F32), pltpu.VMEM((2, RANK, D), F32)],
        cost=(2**24, 12 * 2**20),
    )
    term = call(term_kernel, shape((NZ, ROWS, COL), BF16), basis, gathered, kv_cotangent, error)
    moment, mine, ready = call(
        moment_kernel,
        (shape((2, D, COL)), shape((NX, TOK, 2 * COL), BF16), flag),
        core,
        gathered,
        kv_cotangent,
        error,
        basis,
        specs=[SMEM] + [VMEM] * 4,
        cost=(2 * D * TOK * 2 * COL, 12 * 2**20),
    )
    repeat = functools.partial(repeat_kernel, 1.0)
    term = call(repeat, shape((NY, ROWS, COL)), exchange(term, ("zh", "zl")), ready, cost=(2**20, 12 * 2**20))
    approx, new_error, ready = call(
        final_kernel,
        (shape((2, 64, COL), BF16), shape((2, D, COL), BF16), flag),
        worker,
        exchange(term, ("y",)),
        basis,
        moment,
        specs=[SMEM] + [VMEM] * 3,
        outs=(VMEM, HBM, VMEM),
        scratch=[pltpu.VMEM((COL, 2 * COL), F32), pltpu.VMEM((2, D, COL), BF16), dma((2,))],
    )
    keep, give = call(
        product_kernel,
        (shape((TOK, BLK)), shape((TOK, BLK), BF16)),
        core,
        mine,
        weight,
        ready,
        specs=[SMEM, VMEM, VMEM, VMEM],
        cost=(2 * TOK * D * 2 * COL, 4 * 2**20),
    )
    take = lax.ppermute(give, "core", other_core)
    input_grad = call(add_kernel, shape((TOK, BLK), BF16), keep, take)
    return (input_grad, approx, new_error[None])


def solution(mesh):
    whole = Mesh(mesh.devices.reshape(NY, NH, NL, NX, NC), ("y", "zh", "zl", "x", "core"))
    dp, tensor = ("y", "zh", "zl"), ("x", "core")
    in_specs = (
        P(dp, tensor),
        P(None, dp, tensor),
        P(None, dp, tensor),
        P(dp, None, None, tensor),
        P(None, None, tensor),
    )
    out_specs = (P(dp, tensor), P(None, dp, tensor), P(dp, None, None, tensor))
    return jax.shard_map(shards, mesh=whole, in_specs=in_specs, out_specs=out_specs, check_vma=False)
```

time: 168 us -> 150 us (0.89)
  blocking collectives: 110 us -> 41.4 us
  waiting for transfers between devices: 5.82 us -> 38.7 us
  starting transfers between devices: 11.5 us -> 27.8 us
  Pallas kernels: 12 us -> 15.7 us
  other arithmetic: 1.85 us -> 0 us
    all_to_all x6 -> x3, blocking collectives: 110 us -> 41.4 us  [exchange(): return lax.all_to_all(value, axes, 0, 0, tiled=True)]
    all_to_all x1 -> x3, waiting for transfers between devices: 4.48 us -> 37.3 us  [exchange(): return lax.all_to_all(value, axes, 0, 0, tiled=True)]
    all_to_all x1 -> x3, starting transfers between devices: 3.32 us -> 23.6 us  [exchange(): return lax.all_to_all(value, axes, 0, 0, tiled=True)]
    ppermute x1 -> x2, starting transfers between devices: 8.06 us -> 4.21 us  [the longest x1 3.55 us: shards(): take = lax.ppermute(give, 'core', other_core)]
    pallas_call x9 -> x12, Pallas kernels: 12 us -> 15.7 us  [call(): pl.pallas_call(kernel, out_shape=out_shape, in_specs=specs or [VMEM] * le...]
    unnamed x20 -> x24, local copies, waits for them, and re-layouts: 10.1 us -> 12 us
    concatenate x1 -> x0, other arithmetic: 1.85 us -> none  [shards(): local = jnp.concatenate([normed, kv_cotangent[0], kv_cotangent[1]], axis=1)]
  transfers between devices with their start and end apart: 4 -> 7, of which waited for: 2 -> 4; matrix products, arithmetic and copies ran while one was open for 0% -> 0% of each run, Pallas kernels for 6% -> 7%
where the time goes in v3:
time: 150 us
  blocking collectives  41.4 us (28%)
  waiting for transfers between devices  38.7 us (26%)
  starting transfers between devices  27.8 us (19%)
  Pallas kernels  15.7 us (10%)
  between operations  14.2 us (9%)
  local copies, waits for them, and re-layouts  12 us (8%)
    all_to_all x3, blocking collectives, exchange(): return lax.all_to_all(value, axes, 0, 0, tiled=True)  41.4 us
    all_to_all x3, waiting for transfers between devices, exchange(): return lax.all_to_all(value, axes, 0, 0, tiled=True)  37.3 us
    all_to_all x3, starting transfers between devices, exchange(): return lax.all_to_all(value, axes, 0, 0, tiled=True)  23.6 us
    pallas_call x12, Pallas kernels, call(): pl.pallas_call(kernel, out_shape=out_shape, in_specs=specs or [VMEM] * le...  15.7 us
    unnamed x24, local copies, waits for them, and re-layouts  12 us
    ppermute x1, starting transfers between devices, shards(): take = lax.ppermute(give, 'core', other_core)  3.55 us
  transfers between devices with their start and end apart: 7, of which 4 were waited for; matrix products, arithmetic and copies ran while one was open for 0% of the time, Pallas kernels for 7%

profile of v3, /device:TPU:1, one launch (start us, length us, event | category | flops | bytes accessed | tf_op | source)
XLA Modules:
  0.0 149.7 jit_solution(14794380427623711824)
XLA Ops:
  7.2 3.3 %shard_map.76 = (f32[8,224,128]{2,1,0:T(8,128)}, bf16[6,368,128]{2,1,0:T(8,128)(2,1)}) custom-call(bf16[2,4096,128]{2,1,0:T(8,128)(2,1)} %bitcast.9, bf16[368,512]{1,0:T(8,128)(2,1)} %normed_ref.1, bf16[2,368,128]{2,1,0:T(8,128)(2,1)} %cot_ref.3, f32[2,16,128]{2,1,0:T(8,128)} %q_hbm), custom_call_target="tpu_custom_call" | custom-call | tf_op jit(solution)/shard_map/pallas_call | solution.py:50
  10.6 10.3 %all-to-all-start = ((f32[8,224,128]{2,1,0:T(8,128)}), f32[8,224,128]{2,1,0:T(8,128)S(1)}, u32[]{:S(2)}, u32[]{:S(2)}) async-start(f32[8,224,128]{2,1,0:T(8,128)} %get-tuple-element.21), calls=%async_computation | async-start | bytes 1835008 | tf_op jit(solution)/shard_map/all_to_all | solution.py:275
  21.7 13.1 %all-to-all-done.recv_ref = f32[8,224,128]{2,1,0:T(8,128)S(1)} async-done(((f32[8,224,128]{2,1,0:T(8,128)}), f32[8,224,128]{2,1,0:T(8,128)S(1)}, u32[]{:S(2)}, u32[]{:S(2)}) %all-to-all-start) | async-done | bytes 917536 | tf_op jit(solution)/shard_map/all_to_all | solution.py:275
  34.9 15.3 %all_to_all.30.recv_ref = f32[8,160,128]{2,1,0:T(8,128)S(1)} all-to-all(f32[8,160,128]{2,1,0:T(8,128)S(1)} %shard_map.77), channel_id=1, replica_groups=mesh['y'=4,'zh'=8,'zl'=2,'x'=4,'core'=2] {'y','zl'}, dimensions={0} | all-to-all | bytes 1310720 | tf_op jit(solution)/shard_map/all_to_all | solution.py:275
  51.1 9.7 %all-to-all-start.2 = ((f32[8,32,128]{2,1,0:T(8,128)}), f32[8,32,128]{2,1,0:T(8,128)S(1)}, u32[]{:S(2)}, u32[]{:S(2)}) async-start(f32[8,32,128]{2,1,0:T(8,128)} %get-tuple-element.22), calls=%async_computation.2 | async-start | bytes 262144 | tf_op jit(solution)/shard_map/all_to_all | solution.py:275
  61.4 12.5 %all-to-all-done.2.recv_ref = f32[8,32,128]{2,1,0:T(8,128)S(1)} async-done(((f32[8,32,128]{2,1,0:T(8,128)}), f32[8,32,128]{2,1,0:T(8,128)S(1)}, u32[]{:S(2)}, u32[]{:S(2)}) %all-to-all-start.2) | async-done | bytes 131104 | tf_op jit(solution)/shard_map/all_to_all | solution.py:275
  74.6 19.2 %all_to_all.31.recv_ref = f32[32,32,128]{2,1,0:T(8,128)S(1)} all-to-all(f32[32,32,128]{2,1,0:T(8,128)S(1)} %shard_map.80), channel_id=1, replica_groups=mesh['y'=4,'zh'=8,'zl'=2,'x'=4,'core'=2] {'y','x','core'}, dimensions={0} | all-to-all | bytes 1048576 | tf_op jit(solution)/shard_map/all_to_all | solution.py:275
  93.8 2.8 %shard_map.81.after_ref.basis_ref = f32[2,16,4096]{2,1,0:T(8,128)S(1)} custom-call(f32[32,32,128]{2,1,0:T(8,128)S(1)} %all_to_all.31.recv_ref), custom_call_target="tpu_custom_call" | custom-call | flops 16777216 | bytes 12582912 | tf_op jit(solution)/shard_map/pallas_call | solution.py:50
  96.6 2.3 %copy-done = bf16[48,368,128]{2,1,0:T(8,128)(2,1)S(1)} copy-done((bf16[48,368,128]{2,1,0:T(8,128)(2,1)S(1)}, bf16[48,368,128]{2,1,0:T(8,128)(2,1)}, u32[]{:S(2)}) %copy-start) | copy-done | bytes 4522008
  98.9 2.3 %shard_map.83 = bf16[16,32,128]{2,1,0:T(8,128)(2,1)} custom-call(f32[2,16,4096]{2,1,0:T(8,128)S(1)} %shard_map.81.after_ref.basis_ref, bf16[8,6,368,128]{3,2,1,0:T(8,128)(2,1)S(1)} %bitcast.7, bf16[2,368,128]{2,1,0:T(8,128)(2,1)S(1)} %copy-done.5, bf16[2,4096,128]{2,1,0:T(8,128)(2,1)S(1)} %bitcast.10), custom_call_target="tpu_custom_call" | custom-call | tf_op jit(solution)/shard_map/pallas_call | solution.py:50
  101.3 3.5 %all-to-all-start.4 = ((bf16[16,32,128]{2,1,0:T(8,128)(2,1)}), bf16[16,32,128]{2,1,0:T(8,128)(2,1)S(1)}, u32[]{:S(2)}, u32[]{:S(2)}) async-start(bf16[16,32,128]{2,1,0:T(8,128)(2,1)} %shard_map.83), calls=%async_computation.4 | async-start | bytes 262144 | tf_op jit(solution)/shard_map/all_to_all | solution.py:275
  104.8 2.3 %copy-done.1 = bf16[48,368,128]{2,1,0:T(8,128)(2,1)S(1)} copy-done((bf16[48,368,128]{2,1,0:T(8,128)(2,1)S(1)}, bf16[48,368,128]{2,1,0:T(8,128)(2,1)}, u32[]{:S(2)}) %copy-start.1) | copy-done | bytes 4522008
  107.1 1.3 shard_map.82
  108.5 2.0 %copy-done.3 = f32[2,4096,128]{2,1,0:T(8,128)} copy-done((f32[2,4096,128]{2,1,0:T(8,128)}, f32[2,4096,128]{2,1,0:T(8,128)S(1)}, u32[]{:S(2)}) %copy-start.3) | copy-done | bytes 4194328
  110.5 0.9 copy-done.9
  111.3 11.8 %all-to-all-done.4.recv_ref = bf16[16,32,128]{2,1,0:T(8,128)(2,1)S(1)} async-done(((bf16[16,32,128]{2,1,0:T(8,128)(2,1)}), bf16[16,32,128]{2,1,0:T(8,128)(2,1)S(1)}, u32[]{:S(2)}, u32[]{:S(2)}) %all-to-all-start.4) | async-done | bytes 131104 | tf_op jit(solution)/shard_map/all_to_all | solution.py:275
  123.1 6.8 %all_to_all.32.recv_ref = f32[4,32,128]{2,1,0:T(8,128)S(1)} all-to-all(f32[4,32,128]{2,1,0:T(8,128)S(1)} %shard_map.84), channel_id=1, replica_groups=mesh['y'=4,'zh'=8,'zl'=2,'x'=4,'core'=2] {'y'}, dimensions={0} | all-to-all | bytes 131072 | tf_op jit(solution)/shard_map/all_to_all | solution.py:275
  130.0 2.2 %copy-done.4 = f32[2,4096,128]{2,1,0:T(8,128)S(1)} copy-done((f32[2,4096,128]{2,1,0:T(8,128)S(1)}, f32[2,4096,128]{2,1,0:T(8,128)}, u32[]{:S(2)}) %copy-start.4) | copy-done | bytes 4194328
  132.2 2.5 %shard_map.85 = (bf16[2,64,128]{2,1,0:T(8,128)(2,1)}, bf16[2,4096,128]{2,1,0:T(8,128)(2,1)}, f32[8,128]{1,0:T(8,128)S(1)}) custom-call(s32[1]{0:T(128)} %bitcast.1.worker_ref, f32[4,32,128]{2,1,0:T(8,128)S(1)} %all_to_all.32.recv_ref, f32[2,16,4096]{2,1,0:T(8,128)S(1)} %shard_map.81.after_ref.basis_ref, f32[2,4096,128]{2,1,0:T(8,128)S(1)} %copy-done.4), custom_call_target="tpu_custom_call" | custom-call | tf_op jit(solution)/shard_map/pallas_call | solution.py:50
  134.7 1.6 %copy-done.8 = bf16[64,128,128]{2,1,0:T(8,128)(2,1)S(1)} copy-done((bf16[64,128,128]{2,1,0:T(8,128)(2,1)S(1)}, bf16[64,128,128]{2,1,0:T(8,128)(2,1)}, u32[]{:S(2)}) %copy-start.8) | copy-done | bytes 2097176
  136.3 1.0 shard_map.86
  137.2 3.5 %collective-permute-start.1 = (bf16[368,512]{1,0:T(8,128)(2,1)S(1)}, bf16[368,512]{1,0:T(8,128)(2,1)S(1)}, u32[]{:S(2)}, u32[]{:S(2)}) collective-permute-start(bf16[368,512]{1,0:T(8,128)(2,1)S(1)} %get-tuple-element.30), channel_id=1, source_target_pairs={{0,1},{1,0},{2,3},{3,2},{4,5},{5,4},{6,7},{7,6},{8,9},{9,8},{10,11... | collective-permute-start | bytes 1130504 | tf_op jit(solution)/shard_map/ppermute | solution.py:356
  140.8 1.3 collective-permute-done.1.take_ref
  142.1 0.8 shard_map.87
  (31 shorter events, 3.2 us)
Async XLA Ops:
  7.2 53.6 %all-gather.5.cloned.1.call-start = ((), (), s32[]{:S(2)}) async-start(), calls=%async_computation.6 | async-start | bytes 5087232 | tf_op jit(solution)/shard_map/all_gather | solution.py:305
  7.2 13.7 %copy-start.11 = (bf16[2,64,128]{2,1,0:T(8,128)(2,1)S(1)}, bf16[2,64,128]{2,1,0:T(8,128)(2,1)}, u32[]{:S(2)}) copy-start(bf16[2,64,128]{2,1,0:T(8,128)(2,1)} %param.7) | copy-start | bytes 98308
  7.2 27.5 %copy-start.6 = (bf16[368,512]{1,0:T(8,128)(2,1)S(1)}, bf16[368,512]{1,0:T(8,128)(2,1)}, u32[]{:S(2)}) copy-start(bf16[368,512]{1,0:T(8,128)(2,1)} %normed_ref.1) | copy-start | bytes 1130500
  10.6 24.1 %all-to-all-start = ((f32[8,224,128]{2,1,0:T(8,128)}), f32[8,224,128]{2,1,0:T(8,128)S(1)}, u32[]{:S(2)}, u32[]{:S(2)}) async-start(f32[8,224,128]{2,1,0:T(8,128)} %get-tuple-element.21), calls=%async_computation | async-start | bytes 1835008 | tf_op jit(solution)/shard_map/all_to_all | solution.py:275
  21.0 113.7 %all-gather.7.cloned.1.call-start = ((), (), s32[]{:S(2)}) async-start(), calls=%async_computation.7 | async-start | bytes 2359296 | tf_op jit(solution)/shard_map/all_gather | solution.py:311
  21.0 0.7 collective-permute-start
  51.1 22.8 %all-to-all-start.2 = ((f32[8,32,128]{2,1,0:T(8,128)}), f32[8,32,128]{2,1,0:T(8,128)S(1)}, u32[]{:S(2)}, u32[]{:S(2)}) async-start(f32[8,32,128]{2,1,0:T(8,128)} %get-tuple-element.22), calls=%async_computation.2 | async-start | bytes 262144 | tf_op jit(solution)/shard_map/all_to_all | solution.py:275
  61.4 35.2 %copy-start.2 = (bf16[1,2,4096,128]{3,2,1,0:T(8,128)(2,1)S(1)}, bf16[1,2,4096,128]{3,2,1,0:T(8,128)(2,1)}, u32[]{:S(2)}) copy-start(bf16[1,2,4096,128]{3,2,1,0:T(8,128)(2,1)} %param.8) | copy-start | bytes 6291460
  61.4 35.2 %copy-start.5 = (bf16[2,368,128]{2,1,0:T(8,128)(2,1)S(1)}, bf16[2,368,128]{2,1,0:T(8,128)(2,1)}, u32[]{:S(2)}) copy-start(bf16[2,368,128]{2,1,0:T(8,128)(2,1)} %cot_ref.3) | copy-start | bytes 565252
  73.9 0.7 copy-start.7
  96.6 2.3 %copy-start = (bf16[48,368,128]{2,1,0:T(8,128)(2,1)S(1)}, bf16[48,368,128]{2,1,0:T(8,128)(2,1)}, u32[]{:S(2)}) copy-start(bf16[48,368,128]{2,1,0:T(8,128)(2,1)} %all-gather.5.cloned.1.call-done) | copy-start | bytes 13565956
  101.3 21.8 %all-to-all-start.4 = ((bf16[16,32,128]{2,1,0:T(8,128)(2,1)}), bf16[16,32,128]{2,1,0:T(8,128)(2,1)S(1)}, u32[]{:S(2)}, u32[]{:S(2)}) async-start(bf16[16,32,128]{2,1,0:T(8,128)(2,1)} %shard_map.83), calls=%async_computation.4 | async-start | bytes 262144 | tf_op jit(solution)/shard_map/all_to_all | solution.py:275
  104.8 2.3 %copy-start.1 = (bf16[48,368,128]{2,1,0:T(8,128)(2,1)S(1)}, bf16[48,368,128]{2,1,0:T(8,128)(2,1)}, u32[]{:S(2)}) copy-start(bf16[48,368,128]{2,1,0:T(8,128)(2,1)} %all-gather.5.cloned.1.call-done) | copy-start | bytes 13565956
  108.5 2.0 %copy-start.3 = (f32[2,4096,128]{2,1,0:T(8,128)}, f32[2,4096,128]{2,1,0:T(8,128)S(1)}, u32[]{:S(2)}) copy-start(f32[2,4096,128]{2,1,0:T(8,128)S(1)} %get-tuple-element.27.moment_ref) | copy-start | bytes 12582916
  110.5 0.9 copy-start.9
  130.0 2.2 %copy-start.4 = (f32[2,4096,128]{2,1,0:T(8,128)S(1)}, f32[2,4096,128]{2,1,0:T(8,128)}, u32[]{:S(2)}) copy-start(f32[2,4096,128]{2,1,0:T(8,128)} %copy-done.3) | copy-start | bytes 12582916
  132.2 2.5 %copy-start.10 = (bf16[4,368,256]{2,1,0:T(8,128)(2,1)S(1)}, bf16[4,368,256]{2,1,0:T(8,128)(2,1)}, u32[]{:S(2)}) copy-start(bf16[4,368,256]{2,1,0:T(8,128)(2,1)} %copy-done.9) | copy-start | bytes 2260996
  134.7 1.6 %copy-start.8 = (bf16[64,128,128]{2,1,0:T(8,128)(2,1)S(1)}, bf16[64,128,128]{2,1,0:T(8,128)(2,1)}, u32[]{:S(2)}) copy-start(bf16[64,128,128]{2,1,0:T(8,128)(2,1)} %all-gather.7.cloned.1.call-done) | copy-start | bytes 6291460
  137.2 4.9 %collective-permute-start.1 = (bf16[368,512]{1,0:T(8,128)(2,1)S(1)}, bf16[368,512]{1,0:T(8,128)(2,1)S(1)}, u32[]{:S(2)}, u32[]{:S(2)}) collective-permute-start(bf16[368,512]{1,0:T(8,128)(2,1)S(1)} %get-tuple-element.30), channel_id=1, source_target_pairs={{0,1},{1,0},{2,3},{3,2},{4,5},{5,4},{6,7},{7,6},{8,9},{9,8},{10,11... | collective-permute-start | bytes 1130504 | tf_op jit(solution)/shard_map/ppermute | solution.py:356
Sparse Core Ops, SparseCore 0:
  10.7 46.8 all-gather.4
  60.3 68.3 all-gather.6

commit v4 on v3

--- a/solution.py
+++ b/solution.py
@@ -1,5 +1,3 @@
-import functools
-
 import jax
 import jax.numpy as jnp
 from jax import lax
@@ -13,7 +11,6 @@
 NY, NH, NL, NX, NC = 4, 8, 2, 4, 2
 NT = NX * NC
 NM = NY * NL
-NZ = NH * NL
 BIG = 59 * 2**20
 RANK = 16
 ROWS = 2 * RANK
@@ -128,27 +125,31 @@
     token = jnp.concatenate(pieces(wide(total[4 * ROWS :], ROWS)[:, :TOK], 3), axis=0)
     grad = dot(token, normed_ref[...], NN_DIMS)
     factor = wide(total[: 4 * ROWS], ROWS) + (grad[:ROWS] + grad[ROWS : 2 * ROWS] + grad[2 * ROWS :])
-    weight = [weight_ref[k].astype(F32) for k in range(2)]
     for m in range(NM):
         y = m // NL
-        out_ref[m, :32, :] = tall(factor[8 * y : 8 * y + 8])
+        high, low = pieces(tall(factor[8 * y : 8 * y + 8]), 2)
+        out_ref[m, :32, :] = high
+        out_ref[m, 32:64, :] = low
         for k in range(2):
-            out_ref[m, 32 + 64 * k : 96 + 64 * k, :] = weight[k]
+            out_ref[m, 64 + 64 * k : 128 + 64 * k, :] = weight_ref[k]
 
 
 def third_kernel(recv_ref, out_ref, weight_ref):
-    total = added(recv_ref, slice(0, 32))
+    total = added(recv_ref, slice(0, 32)) + added(recv_ref, slice(32, 64))
     for z in range(NH):
         out_ref[z] = total
     for m in range(NM):
-        weight_ref[m] = recv_ref[m, 32:, :].astype(BF16)
-
-
-def repeat_kernel(scale, recv_ref, after_ref, out_ref):
-    total = added(recv_ref)
-    if scale != 1.0:
-        total = total * scale
-    total = total.astype(out_ref.dtype)
+        weight_ref[m] = recv_ref[m, 64:, :]
+
+
+def repeat_kernel(recv_ref, out_ref):
+    total = added(recv_ref).astype(out_ref.dtype)
+    for i in range(out_ref.shape[0]):
+        out_ref[i] = total
+
+
+def mean_kernel(recv_ref, after_ref, out_ref):
+    total = added(recv_ref) * (1.0 / WORKERS)
     for i in range(out_ref.shape[0]):
         out_ref[i] = total
 
@@ -177,40 +178,30 @@
             v_ref[:, rows, :] = v_ref[:, rows, :] - (coeff * inverse) * column
 
 
-def term_kernel(basis_ref, gathered_ref, cot_ref, error_ref, term_ref):
-    basis = [jnp.concatenate(pieces(basis_ref[k], 3), axis=0) for k in range(2)]
-    both = jnp.concatenate(basis, axis=0)
-    token = jnp.zeros((96, TOK), F32)
-    for t in range(NT):
-        token = token + dot(both[:, block(t)], features(gathered_ref, t), NT_DIMS)
+def term_kernel(basis_ref, high_ref, term_ref):
     for k in range(2):
-        part = token[48 * k : 48 * (k + 1)]
-        part = part[:RANK] + part[RANK : 2 * RANK] + part[2 * RANK :]
-        part = jnp.concatenate(pieces(part, 3), axis=0)
-        term = dot(part, cot_ref[k], NN_DIMS) + dot(basis[k], error_ref[k], NN_DIMS)
+        term = dot(jnp.concatenate(pieces(basis_ref[k], 3), axis=0), high_ref[k], NN_DIMS)
         term = (term[:RANK] + term[RANK : 2 * RANK] + term[2 * RANK :]).astype(BF16)
-        for z in range(NZ):
-            term_ref[z, RANK * k : RANK * (k + 1), :] = term
-
-
-def ready_kernel(gathered_hbm, flag_ref):
-    flag_ref[...] = jnp.zeros((8, 128), F32)
-
-
-def moment_kernel(core_ref, gathered_ref, cot_ref, error_ref, after_ref, moment_ref, mine_ref, flag_ref):
+        for m in range(NM):
+            term_ref[m, RANK * k : RANK * (k + 1), :] = term
+
+
+def moment_kernel(core_ref, gathered_ref, cot_ref, error_ref, high_ref, low_ref, mine_ref, flag_ref):
     flag_ref[...] = jnp.zeros((8, 128), F32)
     cot = jnp.concatenate([cot_ref[0], cot_ref[1]], axis=1)
     for t in range(NT):
         value = dot(features(gathered_ref, t), cot, TN_DIMS)
         for k in range(2):
-            error = error_ref[k, block(t), :].astype(F32)
-            moment_ref[k, block(t), :] = value[:, COL * k : COL * (k + 1)] + error
+            moment = value[:, COL * k : COL * (k + 1)] + error_ref[k, block(t), :].astype(F32)
+            high_ref[k, block(t), :], low_ref[k, block(t), :] = pieces(moment, 2)
     core = core_ref[0]
     for x in range(NX):
         mine_ref[x] = jnp.concatenate([gathered_ref[NC * x + core, 4], gathered_ref[NC * x + core, 5]], axis=1)
 
 
-def final_kernel(worker_ref, recv_ref, basis_ref, moment_ref, approx_ref, new_hbm, flag_ref, tile_ref, new_ref, sems):
+def final_kernel(
+    worker_ref, recv_ref, basis_ref, high_ref, low_ref, approx_ref, new_hbm, flag_ref, tile_ref, new_ref, sems
+):
     flag_ref[...] = jnp.zeros((8, 128), F32)
     parts = [pl.ds(D // 2 * i, D // 2) for i in range(2)]
     q_total = added(recv_ref) * (1.0 / WORKERS)
@@ -239,7 +230,8 @@
     for t in range(NT):
         value = dot(left_of(block(t)), right, TN_DIMS)
         for k in range(2):
-            part = moment_ref[k, block(t), :] - value[:, COL * k : COL * (k + 1)]
+            part = high_ref[k, block(t), :].astype(F32) - value[:, COL * k : COL * (k + 1)]
+            part = part + low_ref[k, block(t), :].astype(F32)
             new_ref[k, block(t), :] = part.astype(BF16)
         if t % 4 == 3:
             done = parts[t // 4]
@@ -284,7 +276,6 @@
 
     swap = [(NX * i + j, NX * j + i) for i in range(NY) for j in range(NX)]
     weight = lax.ppermute(kv_weight, ("y", "x"), swap)
-    flag = shape((8, 128))
     sent, local = call(
         first_kernel,
         (shape((NT, 7 * ROWS, 128)), shape((6, TOK, 128), BF16)),
@@ -303,14 +294,21 @@
         limit=BIG,
     )
     gathered = lax.all_gather(local, ("x", "core"), axis=0, tiled=False)
-    ready = call(ready_kernel, flag, gathered, specs=[HBM], limit=BIG)
-    other_core = [(0, 1), (1, 0)]
     recv = exchange(sent, ("x", "core"))
-    recv = exchange(call(second_kernel, shape((NM, 160, 128)), recv, normed, weight), ("y", "zl"))
+    recv = exchange(call(second_kernel, shape((NM, 192, 128), BF16), recv, normed, weight), ("y", "zl"))
     sent, weight = call(third_kernel, (shape((NH, 32, 128)), shape((NM, 128, 128), BF16)), recv)
     weight = lax.all_gather(weight, "zh", axis=0, tiled=False)
-    mean = functools.partial(repeat_kernel, 1.0 / WORKERS)
-    sent = call(mean, shape((NY * NT, 32, 128)), exchange(sent, ("zh",)), ready)
+    high, low, mine, ready = call(
+        moment_kernel,
+        (shape((2, D, COL), BF16), shape((2, D, COL), BF16), shape((NX, TOK, 2 * COL), BF16), shape((8, 128))),
+        core,
+        gathered,
+        kv_cotangent,
+        error,
+        specs=[SMEM] + [VMEM] * 3,
+        cost=(2 * D * TOK * 2 * COL, 12 * 2**20),
+    )
+    sent = call(mean_kernel, shape((NY * NT, 32, 128)), exchange(sent, ("zh",)), ready)
     basis = call(
         basis_kernel,
         shape((2, RANK, D)),
@@ -318,28 +316,17 @@
         scratch=[pltpu.VMEM((2, RANK, D), F32), pltpu.VMEM((2, RANK, D), F32)],
         cost=(2**24, 12 * 2**20),
     )
-    term = call(term_kernel, shape((NZ, ROWS, COL), BF16), basis, gathered, kv_cotangent, error)
-    moment, mine, ready = call(
-        moment_kernel,
-        (shape((2, D, COL)), shape((NX, TOK, 2 * COL), BF16), flag),
-        core,
-        gathered,
-        kv_cotangent,
-        error,
-        basis,
-        specs=[SMEM] + [VMEM] * 4,
-        cost=(2 * D * TOK * 2 * COL, 12 * 2**20),
-    )
-    repeat = functools.partial(repeat_kernel, 1.0)
-    term = call(repeat, shape((NY, ROWS, COL)), exchange(term, ("zh", "zl")), ready, cost=(2**20, 12 * 2**20))
+    term = call(term_kernel, shape((NM, ROWS, COL), BF16), basis, high)
+    term = call(repeat_kernel, shape((NH, ROWS, COL), BF16), exchange(term, ("y", "zl")))
     approx, new_error, ready = call(
         final_kernel,
-        (shape((2, 64, COL), BF16), shape((2, D, COL), BF16), flag),
+        (shape((2, 64, COL), BF16), shape((2, D, COL), BF16), shape((8, 128))),
         worker,
-        exchange(term, ("y",)),
+        exchange(term, ("zh",)),
         basis,
-        moment,
-        specs=[SMEM] + [VMEM] * 3,
+        high,
+        low,
+        specs=[SMEM] + [VMEM] * 4,
         outs=(VMEM, HBM, VMEM),
         scratch=[pltpu.VMEM((COL, 2 * COL), F32), pltpu.VMEM((2, D, COL), BF16), dma((2,))],
     )
@@ -350,10 +337,10 @@
         mine,
         weight,
         ready,
-        specs=[SMEM, VMEM, VMEM, VMEM],
+        specs=[SMEM] + [VMEM] * 3,
         cost=(2 * TOK * D * 2 * COL, 4 * 2**20),
     )
-    take = lax.ppermute(give, "core", other_core)
+    take = lax.ppermute(give, "core", [(0, 1), (1, 0)])
     input_grad = call(add_kernel, shape((TOK, BLK), BF16), keep, take)
     return (input_grad, approx, new_error[None])
 

time: 150 us -> 142 us (0.947)
  blocking collectives: 41.4 us -> 61.3 us
  waiting for transfers between devices: 38.7 us -> 21.1 us
  local copies, waits for them, and re-layouts: 12 us -> 6.78 us
  starting transfers between devices: 27.8 us -> 24.7 us
  Pallas kernels: 15.7 us -> 13.4 us
    all_to_all x3 -> x4, blocking collectives: 41.4 us -> 61.3 us  [exchange(): return lax.all_to_all(value, axes, 0, 0, tiled=True)]
    all_to_all x3 -> x2, waiting for transfers between devices: 37.3 us -> 19.7 us  [exchange(): return lax.all_to_all(value, axes, 0, 0, tiled=True)]
    unnamed x24 -> x16, local copies, waits for them, and re-layouts: 12 us -> 6.78 us
    all_to_all x3 -> x2, starting transfers between devices: 23.6 us -> 20.1 us  [exchange(): return lax.all_to_all(value, axes, 0, 0, tiled=True)]
    pallas_call x12 -> x11, Pallas kernels: 15.7 us -> 13.4 us  [call(): pl.pallas_call(kernel, out_shape=out_shape, in_specs=specs or [VMEM] * le...]
  transfers between devices with their start and end apart: 7 -> 6, of which waited for: 4 -> 3; matrix products, arithmetic and copies ran while one was open for 0% -> 0% of each run, Pallas kernels for 7% -> 6%
where the time goes in v4:
time: 142 us; the launch traced here: 141 us
  blocking collectives  61.3 us (43%)
  starting transfers between devices  24.7 us (17%)
  waiting for transfers between devices  21.1 us (15%)
  between operations  14.2 us (10%)
  Pallas kernels  13.4 us (9%)
  local copies, waits for them, and re-layouts  6.78 us (5%)
    all_to_all x4, blocking collectives, exchange(): return lax.all_to_all(value, axes, 0, 0, tiled=True)  61.3 us
    all_to_all x2, starting transfers between devices, exchange(): return lax.all_to_all(value, axes, 0, 0, tiled=True)  20.1 us
    all_to_all x2, waiting for transfers between devices, exchange(): return lax.all_to_all(value, axes, 0, 0, tiled=True)  19.7 us
    pallas_call x11, Pallas kernels, call(): pl.pallas_call(kernel, out_shape=out_shape, in_specs=specs or [VMEM] * le...  13.4 us
    unnamed x16, local copies, waits for them, and re-layouts  6.78 us
    ppermute x1, starting transfers between devices, shards(): take = lax.ppermute(give, 'core', [(0, 1), (1, 0)])  3.79 us
  transfers between devices with their start and end apart: 6, of which 3 were waited for; matrix products, arithmetic and copies ran while one was open for 0% of the time, Pallas kernels for 6%

profile of v4, /device:TPU:1, one launch (start us, length us, event | category | flops | bytes accessed | tf_op | source)
XLA Modules:
  0.0 141.4 jit_solution(13265540555361365710)
XLA Ops:
  7.2 3.3 %shard_map.76 = (f32[8,224,128]{2,1,0:T(8,128)}, bf16[6,368,128]{2,1,0:T(8,128)(2,1)}) custom-call(bf16[2,4096,128]{2,1,0:T(8,128)(2,1)} %bitcast.6, bf16[368,512]{1,0:T(8,128)(2,1)} %normed_ref.1, bf16[2,368,128]{2,1,0:T(8,128)(2,1)} %cot_ref.1, f32[2,16,128]{2,1,0:T(8,128)} %q_hbm), custom_call_target="tpu_custom_call" | custom-call | tf_op jit(solution)/shard_map/pallas_call | solution.py:47
  10.6 10.3 %all-to-all-start = ((f32[8,224,128]{2,1,0:T(8,128)}), f32[8,224,128]{2,1,0:T(8,128)S(1)}, u32[]{:S(2)}, u32[]{:S(2)}) async-start(f32[8,224,128]{2,1,0:T(8,128)} %get-tuple-element.23), calls=%async_computation | async-start | bytes 1835008 | tf_op jit(solution)/shard_map/all_to_all | solution.py:267
  21.0 0.8 collective-permute-start
  21.8 12.9 %all-to-all-done.recv_ref = f32[8,224,128]{2,1,0:T(8,128)S(1)} async-done(((f32[8,224,128]{2,1,0:T(8,128)}), f32[8,224,128]{2,1,0:T(8,128)S(1)}, u32[]{:S(2)}, u32[]{:S(2)}) %all-to-all-start) | async-done | bytes 917536 | tf_op jit(solution)/shard_map/all_to_all | solution.py:267
  34.7 0.2 shard_map.78
  35.0 12.4 %all_to_all.30.recv_ref = bf16[8,192,128]{2,1,0:T(8,128)(2,1)S(1)} all-to-all(bf16[8,192,128]{2,1,0:T(8,128)(2,1)S(1)} %shard_map.78), channel_id=1, replica_groups=mesh['y'=4,'zh'=8,'zl'=2,'x'=4,'core'=2] {'y','zl'}, dimensions={0} | all-to-all | bytes 786432 | tf_op jit(solution)/shard_map/all_to_all | solution.py:267
  47.4 0.8 shard_map.79
  48.2 9.8 %all-to-all-start.2 = ((f32[8,32,128]{2,1,0:T(8,128)}), f32[8,32,128]{2,1,0:T(8,128)S(1)}, u32[]{:S(2)}, u32[]{:S(2)}) async-start(f32[8,32,128]{2,1,0:T(8,128)} %get-tuple-element.26), calls=%async_computation.2 | async-start | bytes 262144 | tf_op jit(solution)/shard_map/all_to_all | solution.py:267
  58.0 1.6 %copy-done = bf16[1,2,4096,128]{3,2,1,0:T(8,128)(2,1)S(1)} copy-done((bf16[1,2,4096,128]{3,2,1,0:T(8,128)(2,1)S(1)}, bf16[1,2,4096,128]{3,2,1,0:T(8,128)(2,1)}, u32[]{:S(2)}) %copy-start) | copy-done | bytes 2097176
  59.6 2.3 %copy-done.1 = bf16[48,368,128]{2,1,0:T(8,128)(2,1)S(1)} copy-done((bf16[48,368,128]{2,1,0:T(8,128)(2,1)S(1)}, bf16[48,368,128]{2,1,0:T(8,128)(2,1)}, u32[]{:S(2)}) %copy-start.1) | copy-done | bytes 4522008
  61.8 1.4 %shard_map.77 = (bf16[2,4096,128]{2,1,0:T(8,128)(2,1)S(1)}, bf16[2,4096,128]{2,1,0:T(8,128)(2,1)S(1)}, bf16[4,368,256]{2,1,0:T(8,128)(2,1)S(1)}, f32[8,128]{1,0:T(8,128)S(1)}) custom-call(s32[1]{0:T(128)} %bitcast.core_ref, bf16[8,6,368,128]{3,2,1,0:T(8,128)(2,1)S(1)} %bitcast.8, bf16[2,368,128]{2,1,0:T(8,128)(2,1)S(1)} %copy-done.5, ...), custom_call_target="tpu_custom_call" | custom-call | flops 771751936 | bytes 12582912 | tf_op jit(solution)/shard_map/pallas_call | solution.py:47
  63.3 1.3 copy-done.2
  64.6 6.8 %all-to-all-done.2.recv_ref = f32[8,32,128]{2,1,0:T(8,128)S(1)} async-done(((f32[8,32,128]{2,1,0:T(8,128)}), f32[8,32,128]{2,1,0:T(8,128)S(1)}, u32[]{:S(2)}, u32[]{:S(2)}) %all-to-all-start.2) | async-done | bytes 131104 | tf_op jit(solution)/shard_map/all_to_all | solution.py:267
  71.5 18.8 %all_to_all.31.recv_ref = f32[32,32,128]{2,1,0:T(8,128)S(1)} all-to-all(f32[32,32,128]{2,1,0:T(8,128)S(1)} %shard_map.80), channel_id=1, replica_groups=mesh['y'=4,'zh'=8,'zl'=2,'x'=4,'core'=2] {'y','x','core'}, dimensions={0} | all-to-all | bytes 1048576 | tf_op jit(solution)/shard_map/all_to_all | solution.py:267
  90.3 2.8 %shard_map.81.basis_ref = f32[2,16,4096]{2,1,0:T(8,128)S(1)} custom-call(f32[32,32,128]{2,1,0:T(8,128)S(1)} %all_to_all.31.recv_ref), custom_call_target="tpu_custom_call" | custom-call | flops 16777216 | bytes 12582912 | tf_op jit(solution)/shard_map/pallas_call | solution.py:47
  93.1 0.5 shard_map.82
  93.5 11.7 %all_to_all.32.recv_ref = bf16[8,32,128]{2,1,0:T(8,128)(2,1)S(1)} all-to-all(bf16[8,32,128]{2,1,0:T(8,128)(2,1)S(1)} %shard_map.82), channel_id=1, replica_groups=mesh['y'=4,'zh'=8,'zl'=2,'x'=4,'core'=2] {'y','zl'}, dimensions={0} | all-to-all | bytes 131072 | tf_op jit(solution)/shard_map/all_to_all | solution.py:267
  105.2 18.3 %all_to_all.33.recv_ref = bf16[8,32,128]{2,1,0:T(8,128)(2,1)S(1)} all-to-all(bf16[8,32,128]{2,1,0:T(8,128)(2,1)S(1)} %shard_map.83), channel_id=1, replica_groups=mesh['y'=4,'zh'=8,'zl'=2,'x'=4,'core'=2] {'zh'}, dimensions={0} | all-to-all | bytes 131072 | tf_op jit(solution)/shard_map/all_to_all | solution.py:267
  123.5 2.5 %shard_map.84 = (bf16[2,64,128]{2,1,0:T(8,128)(2,1)}, bf16[2,4096,128]{2,1,0:T(8,128)(2,1)}, f32[8,128]{1,0:T(8,128)S(1)}) custom-call(s32[1]{0:T(128)} %bitcast.1.worker_ref, bf16[8,32,128]{2,1,0:T(8,128)(2,1)S(1)} %all_to_all.33.recv_ref, f32[2,16,4096]{2,1,0:T(8,128)S(1)} %shard_map.81.basis_ref, bf16[2,4096,128]{2,1,0:T(8,128)(2,1)S(1)} %get-tuple-element.28.high_ref, ...), custom_call_target="tpu_custom_call" | custom-call | tf_op jit(solution)/shard_map/pallas_call | solution.py:47
  126.1 1.6 %copy-done.6 = bf16[64,128,128]{2,1,0:T(8,128)(2,1)S(1)} copy-done((bf16[64,128,128]{2,1,0:T(8,128)(2,1)S(1)}, bf16[64,128,128]{2,1,0:T(8,128)(2,1)}, u32[]{:S(2)}) %copy-start.6) | copy-done | bytes 2097176
  127.7 1.0 shard_map.85
  128.7 3.8 %collective-permute-start.1 = (bf16[368,512]{1,0:T(8,128)(2,1)S(1)}, bf16[368,512]{1,0:T(8,128)(2,1)S(1)}, u32[]{:S(2)}, u32[]{:S(2)}) collective-permute-start(bf16[368,512]{1,0:T(8,128)(2,1)S(1)} %get-tuple-element.32), channel_id=1, source_target_pairs={{0,1},{1,0},{2,3},{3,2},{4,5},{5,4},{6,7},{7,6},{8,9},{9,8},{10,11... | collective-permute-start | bytes 1130504 | tf_op jit(solution)/shard_map/ppermute | solution.py:343
  132.5 1.3 collective-permute-done.1.take_ref
  133.8 0.8 shard_map.86
  (21 shorter events, 0.2 us)
Async XLA Ops:
  7.2 50.8 %all-gather.5.cloned.1.call-start = ((), (), s32[]{:S(2)}) async-start(), calls=%async_computation.6 | async-start | bytes 5087232 | tf_op jit(solution)/shard_map/all_gather | solution.py:296
  7.2 13.7 %copy-start.7 = (bf16[2,64,128]{2,1,0:T(8,128)(2,1)S(1)}, bf16[2,64,128]{2,1,0:T(8,128)(2,1)}, u32[]{:S(2)}) copy-start(bf16[2,64,128]{2,1,0:T(8,128)(2,1)} %param.7) | copy-start | bytes 98308
  7.2 27.5 %copy-start.4 = (bf16[368,512]{1,0:T(8,128)(2,1)S(1)}, bf16[368,512]{1,0:T(8,128)(2,1)}, u32[]{:S(2)}) copy-start(bf16[368,512]{1,0:T(8,128)(2,1)} %normed_ref.1) | copy-start | bytes 1130500
  10.6 24.1 %all-to-all-start = ((f32[8,224,128]{2,1,0:T(8,128)}), f32[8,224,128]{2,1,0:T(8,128)S(1)}, u32[]{:S(2)}, u32[]{:S(2)}) async-start(f32[8,224,128]{2,1,0:T(8,128)} %get-tuple-element.23), calls=%async_computation | async-start | bytes 1835008 | tf_op jit(solution)/shard_map/all_to_all | solution.py:267
  21.0 37.0 %copy-start.5 = (bf16[2,368,128]{2,1,0:T(8,128)(2,1)S(1)}, bf16[2,368,128]{2,1,0:T(8,128)(2,1)}, u32[]{:S(2)}) copy-start(bf16[2,368,128]{2,1,0:T(8,128)(2,1)} %cot_ref.1) | copy-start | bytes 565252
  21.0 105.2 %all-gather.7.cloned.1.call-start = ((), (), s32[]{:S(2)}) async-start(), calls=%async_computation.7 | async-start | bytes 2359296 | tf_op jit(solution)/shard_map/all_gather | solution.py:300
  21.0 0.8 collective-permute-start
  48.2 23.2 %all-to-all-start.2 = ((f32[8,32,128]{2,1,0:T(8,128)}), f32[8,32,128]{2,1,0:T(8,128)S(1)}, u32[]{:S(2)}, u32[]{:S(2)}) async-start(f32[8,32,128]{2,1,0:T(8,128)} %get-tuple-element.26), calls=%async_computation.2 | async-start | bytes 262144 | tf_op jit(solution)/shard_map/all_to_all | solution.py:267
  58.0 1.6 %copy-start = (bf16[1,2,4096,128]{3,2,1,0:T(8,128)(2,1)S(1)}, bf16[1,2,4096,128]{3,2,1,0:T(8,128)(2,1)}, u32[]{:S(2)}) copy-start(bf16[1,2,4096,128]{3,2,1,0:T(8,128)(2,1)} %param.8) | copy-start | bytes 6291460
  59.6 2.3 %copy-start.1 = (bf16[48,368,128]{2,1,0:T(8,128)(2,1)S(1)}, bf16[48,368,128]{2,1,0:T(8,128)(2,1)}, u32[]{:S(2)}) copy-start(bf16[48,368,128]{2,1,0:T(8,128)(2,1)} %all-gather.5.cloned.1.call-done) | copy-start | bytes 13565956
  63.3 1.3 copy-start.2
  90.3 33.2 %copy-start.3 = (bf16[2,4096,128]{2,1,0:T(8,128)(2,1)S(1)}, bf16[2,4096,128]{2,1,0:T(8,128)(2,1)}, u32[]{:S(2)}) copy-start(bf16[2,4096,128]{2,1,0:T(8,128)(2,1)} %copy-done.2) | copy-start | bytes 6291460
  126.1 1.6 %copy-start.6 = (bf16[64,128,128]{2,1,0:T(8,128)(2,1)S(1)}, bf16[64,128,128]{2,1,0:T(8,128)(2,1)}, u32[]{:S(2)}) copy-start(bf16[64,128,128]{2,1,0:T(8,128)(2,1)} %all-gather.7.cloned.1.call-done) | copy-start | bytes 6291460
  128.7 5.1 %collective-permute-start.1 = (bf16[368,512]{1,0:T(8,128)(2,1)S(1)}, bf16[368,512]{1,0:T(8,128)(2,1)S(1)}, u32[]{:S(2)}, u32[]{:S(2)}) collective-permute-start(bf16[368,512]{1,0:T(8,128)(2,1)S(1)} %get-tuple-element.32), channel_id=1, source_target_pairs={{0,1},{1,0},{2,3},{3,2},{4,5},{5,4},{6,7},{7,6},{8,9},{9,8},{10,11... | collective-permute-start | bytes 1130504 | tf_op jit(solution)/shard_map/ppermute | solution.py:343
Sparse Core Ops, SparseCore 0:
  10.7 46.8 all-gather.4
  60.3 65.5 all-gather.6

commit v5 on v4

--- a/solution.py
+++ b/solution.py
@@ -136,8 +136,10 @@
 
 def third_kernel(recv_ref, out_ref, weight_ref):
     total = added(recv_ref, slice(0, 32)) + added(recv_ref, slice(32, 64))
+    high, low = pieces(total, 2)
     for z in range(NH):
-        out_ref[z] = total
+        out_ref[z, :32, :] = high
+        out_ref[z, 32:, :] = low
     for m in range(NM):
         weight_ref[m] = recv_ref[m, 64:, :]
 
@@ -149,9 +151,11 @@
 
 
 def mean_kernel(recv_ref, after_ref, out_ref):
-    total = added(recv_ref) * (1.0 / WORKERS)
+    total = (added(recv_ref, slice(0, 32)) + added(recv_ref, slice(32, 64))) * (1.0 / WORKERS)
+    high, low = pieces(total, 2)
     for i in range(out_ref.shape[0]):
-        out_ref[i] = total
+        out_ref[i, :32, :] = high
+        out_ref[i, 32:, :] = low
 
 
 def features(gathered_ref, t):
@@ -162,7 +166,8 @@
     for y in range(NY):
         rows = slice(8 * (y % 2), 8 * (y % 2) + 8)
         for t in range(NT):
-            value = wide(recv_ref[NT * y + t], 8)
+            place = NT * y + t
+            value = wide(recv_ref[place, :32].astype(F32) + recv_ref[place, 32:].astype(F32), 8)
             p_ref[y // 2, rows, block(t)] = value
             v_ref[y // 2, rows, block(t)] = value
     for i in range(RANK):
@@ -296,7 +301,7 @@
     gathered = lax.all_gather(local, ("x", "core"), axis=0, tiled=False)
     recv = exchange(sent, ("x", "core"))
     recv = exchange(call(second_kernel, shape((NM, 192, 128), BF16), recv, normed, weight), ("y", "zl"))
-    sent, weight = call(third_kernel, (shape((NH, 32, 128)), shape((NM, 128, 128), BF16)), recv)
+    sent, weight = call(third_kernel, (shape((NH, 64, 128), BF16), shape((NM, 128, 128), BF16)), recv)
     weight = lax.all_gather(weight, "zh", axis=0, tiled=False)
     high, low, mine, ready = call(
         moment_kernel,
@@ -308,7 +313,7 @@
         specs=[SMEM] + [VMEM] * 3,
         cost=(2 * D * TOK * 2 * COL, 12 * 2**20),
     )
-    sent = call(mean_kernel, shape((NY * NT, 32, 128)), exchange(sent, ("zh",)), ready)
+    sent = call(mean_kernel, shape((NY * NT, 64, 128), BF16), exchange(sent, ("zh",)), ready)
     basis = call(
         basis_kernel,
         shape((2, RANK, D)),

time: 142 us -> 142 us (level)
  no operation moved by 1% of the time
where the time goes in v5:
time: 142 us
  blocking collectives  61.4 us (43%)
  starting transfers between devices  24.7 us (17%)
  waiting for transfers between devices  21.1 us (15%)
  between operations  14.2 us (10%)
  Pallas kernels  13.4 us (9%)
  local copies, waits for them, and re-layouts  6.78 us (5%)
    all_to_all x4, blocking collectives, exchange(): return lax.all_to_all(value, axes, 0, 0, tiled=True)  61.4 us
    all_to_all x2, starting transfers between devices, exchange(): return lax.all_to_all(value, axes, 0, 0, tiled=True)  20.1 us
    all_to_all x2, waiting for transfers between devices, exchange(): return lax.all_to_all(value, axes, 0, 0, tiled=True)  19.7 us
    pallas_call x11, Pallas kernels, call(): pl.pallas_call(kernel, out_shape=out_shape, in_specs=specs or [VMEM] * le...  13.4 us
    unnamed x16, local copies, waits for them, and re-layouts  6.78 us
    ppermute x1, starting transfers between devices, shards(): take = lax.ppermute(give, 'core', [(0, 1), (1, 0)])  3.74 us
  transfers between devices with their start and end apart: 6, of which 3 were waited for; matrix products, arithmetic and copies ran while one was open for 0% of the time, Pallas kernels for 6%

profile of v5, /device:TPU:1, one launch (start us, length us, event | category | flops | bytes accessed | tf_op | source)
XLA Modules:
  0.0 141.6 jit_solution(13034424089621666429)
XLA Ops:
  7.2 3.3 %shard_map.76 = (f32[8,224,128]{2,1,0:T(8,128)}, bf16[6,368,128]{2,1,0:T(8,128)(2,1)}) custom-call(bf16[2,4096,128]{2,1,0:T(8,128)(2,1)} %bitcast.6, bf16[368,512]{1,0:T(8,128)(2,1)} %normed_ref.1, bf16[2,368,128]{2,1,0:T(8,128)(2,1)} %cot_ref.1, f32[2,16,128]{2,1,0:T(8,128)} %q_hbm), custom_call_target="tpu_custom_call" | custom-call | tf_op jit(solution)/shard_map/pallas_call | solution.py:47
  10.6 10.3 %all-to-all-start = ((f32[8,224,128]{2,1,0:T(8,128)}), f32[8,224,128]{2,1,0:T(8,128)S(1)}, u32[]{:S(2)}, u32[]{:S(2)}) async-start(f32[8,224,128]{2,1,0:T(8,128)} %get-tuple-element.23), calls=%async_computation | async-start | bytes 1835008 | tf_op jit(solution)/shard_map/all_to_all | solution.py:272
  21.0 0.8 collective-permute-start
  21.8 12.9 %all-to-all-done.recv_ref = f32[8,224,128]{2,1,0:T(8,128)S(1)} async-done(((f32[8,224,128]{2,1,0:T(8,128)}), f32[8,224,128]{2,1,0:T(8,128)S(1)}, u32[]{:S(2)}, u32[]{:S(2)}) %all-to-all-start) | async-done | bytes 917536 | tf_op jit(solution)/shard_map/all_to_all | solution.py:272
  34.7 0.2 shard_map.78
  35.0 12.4 %all_to_all.30.recv_ref = bf16[8,192,128]{2,1,0:T(8,128)(2,1)S(1)} all-to-all(bf16[8,192,128]{2,1,0:T(8,128)(2,1)S(1)} %shard_map.78), channel_id=1, replica_groups=mesh['y'=4,'zh'=8,'zl'=2,'x'=4,'core'=2] {'y','zl'}, dimensions={0} | all-to-all | bytes 786432 | tf_op jit(solution)/shard_map/all_to_all | solution.py:272
  47.4 0.8 shard_map.79
  48.2 9.8 %all-to-all-start.2 = ((bf16[8,64,128]{2,1,0:T(8,128)(2,1)}), bf16[8,64,128]{2,1,0:T(8,128)(2,1)S(1)}, u32[]{:S(2)}, u32[]{:S(2)}) async-start(bf16[8,64,128]{2,1,0:T(8,128)(2,1)} %get-tuple-element.26), calls=%async_computation.2 | async-start | bytes 262144 | tf_op jit(solution)/shard_map/all_to_all | solution.py:272
  58.0 1.6 %copy-done = bf16[1,2,4096,128]{3,2,1,0:T(8,128)(2,1)S(1)} copy-done((bf16[1,2,4096,128]{3,2,1,0:T(8,128)(2,1)S(1)}, bf16[1,2,4096,128]{3,2,1,0:T(8,128)(2,1)}, u32[]{:S(2)}) %copy-start) | copy-done | bytes 2097176
  59.6 2.3 %copy-done.1 = bf16[48,368,128]{2,1,0:T(8,128)(2,1)S(1)} copy-done((bf16[48,368,128]{2,1,0:T(8,128)(2,1)S(1)}, bf16[48,368,128]{2,1,0:T(8,128)(2,1)}, u32[]{:S(2)}) %copy-start.1) | copy-done | bytes 4522008
  61.8 1.4 %shard_map.77 = (bf16[2,4096,128]{2,1,0:T(8,128)(2,1)S(1)}, bf16[2,4096,128]{2,1,0:T(8,128)(2,1)S(1)}, bf16[4,368,256]{2,1,0:T(8,128)(2,1)S(1)}, f32[8,128]{1,0:T(8,128)S(1)}) custom-call(s32[1]{0:T(128)} %bitcast.core_ref, bf16[8,6,368,128]{3,2,1,0:T(8,128)(2,1)S(1)} %bitcast.8, bf16[2,368,128]{2,1,0:T(8,128)(2,1)S(1)} %copy-done.5, ...), custom_call_target="tpu_custom_call" | custom-call | flops 771751936 | bytes 12582912 | tf_op jit(solution)/shard_map/pallas_call | solution.py:47
  63.3 1.3 copy-done.2
  64.6 6.8 %all-to-all-done.2.recv_ref = bf16[8,64,128]{2,1,0:T(8,128)(2,1)S(1)} async-done(((bf16[8,64,128]{2,1,0:T(8,128)(2,1)}), bf16[8,64,128]{2,1,0:T(8,128)(2,1)S(1)}, u32[]{:S(2)}, u32[]{:S(2)}) %all-to-all-start.2) | async-done | bytes 131104 | tf_op jit(solution)/shard_map/all_to_all | solution.py:272
  71.5 18.8 %all_to_all.31.recv_ref = bf16[32,64,128]{2,1,0:T(8,128)(2,1)S(1)} all-to-all(bf16[32,64,128]{2,1,0:T(8,128)(2,1)S(1)} %shard_map.80), channel_id=1, replica_groups=mesh['y'=4,'zh'=8,'zl'=2,'x'=4,'core'=2] {'y','x','core'}, dimensions={0} | all-to-all | bytes 1048576 | tf_op jit(solution)/shard_map/all_to_all | solution.py:272
  90.3 2.8 %shard_map.81.basis_ref = f32[2,16,4096]{2,1,0:T(8,128)S(1)} custom-call(bf16[32,64,128]{2,1,0:T(8,128)(2,1)S(1)} %all_to_all.31.recv_ref), custom_call_target="tpu_custom_call" | custom-call | flops 16777216 | bytes 12582912 | tf_op jit(solution)/shard_map/pallas_call | solution.py:47
  93.1 0.5 shard_map.82
  93.6 11.7 %all_to_all.32.recv_ref = bf16[8,32,128]{2,1,0:T(8,128)(2,1)S(1)} all-to-all(bf16[8,32,128]{2,1,0:T(8,128)(2,1)S(1)} %shard_map.82), channel_id=1, replica_groups=mesh['y'=4,'zh'=8,'zl'=2,'x'=4,'core'=2] {'y','zl'}, dimensions={0} | all-to-all | bytes 131072 | tf_op jit(solution)/shard_map/all_to_all | solution.py:272
  105.2 18.5 %all_to_all.33.recv_ref = bf16[8,32,128]{2,1,0:T(8,128)(2,1)S(1)} all-to-all(bf16[8,32,128]{2,1,0:T(8,128)(2,1)S(1)} %shard_map.83), channel_id=1, replica_groups=mesh['y'=4,'zh'=8,'zl'=2,'x'=4,'core'=2] {'zh'}, dimensions={0} | all-to-all | bytes 131072 | tf_op jit(solution)/shard_map/all_to_all | solution.py:272
  123.7 2.5 %shard_map.84 = (bf16[2,64,128]{2,1,0:T(8,128)(2,1)}, bf16[2,4096,128]{2,1,0:T(8,128)(2,1)}, f32[8,128]{1,0:T(8,128)S(1)}) custom-call(s32[1]{0:T(128)} %bitcast.1.worker_ref, bf16[8,32,128]{2,1,0:T(8,128)(2,1)S(1)} %all_to_all.33.recv_ref, f32[2,16,4096]{2,1,0:T(8,128)S(1)} %shard_map.81.basis_ref, bf16[2,4096,128]{2,1,0:T(8,128)(2,1)S(1)} %get-tuple-element.28.high_ref, ...), custom_call_target="tpu_custom_call" | custom-call | tf_op jit(solution)/shard_map/pallas_call | solution.py:47
  126.3 1.6 %copy-done.6 = bf16[64,128,128]{2,1,0:T(8,128)(2,1)S(1)} copy-done((bf16[64,128,128]{2,1,0:T(8,128)(2,1)S(1)}, bf16[64,128,128]{2,1,0:T(8,128)(2,1)}, u32[]{:S(2)}) %copy-start.6) | copy-done | bytes 2097176
  127.9 1.0 shard_map.85
  128.9 3.7 %collective-permute-start.1 = (bf16[368,512]{1,0:T(8,128)(2,1)S(1)}, bf16[368,512]{1,0:T(8,128)(2,1)S(1)}, u32[]{:S(2)}, u32[]{:S(2)}) collective-permute-start(bf16[368,512]{1,0:T(8,128)(2,1)S(1)} %get-tuple-element.32), channel_id=1, source_target_pairs={{0,1},{1,0},{2,3},{3,2},{4,5},{5,4},{6,7},{7,6},{8,9},{9,8},{10,11... | collective-permute-start | bytes 1130504 | tf_op jit(solution)/shard_map/ppermute | solution.py:348
  132.6 1.3 collective-permute-done.1.take_ref
  133.9 0.8 shard_map.86
  (21 shorter events, 0.2 us)
Async XLA Ops:
  7.2 50.8 %all-gather.5.cloned.1.call-start = ((), (), s32[]{:S(2)}) async-start(), calls=%async_computation.6 | async-start | bytes 5087232 | tf_op jit(solution)/shard_map/all_gather | solution.py:301
  7.2 13.7 %copy-start.7 = (bf16[2,64,128]{2,1,0:T(8,128)(2,1)S(1)}, bf16[2,64,128]{2,1,0:T(8,128)(2,1)}, u32[]{:S(2)}) copy-start(bf16[2,64,128]{2,1,0:T(8,128)(2,1)} %param.7) | copy-start | bytes 98308
  7.2 27.5 %copy-start.4 = (bf16[368,512]{1,0:T(8,128)(2,1)S(1)}, bf16[368,512]{1,0:T(8,128)(2,1)}, u32[]{:S(2)}) copy-start(bf16[368,512]{1,0:T(8,128)(2,1)} %normed_ref.1) | copy-start | bytes 1130500
  10.6 24.1 %all-to-all-start = ((f32[8,224,128]{2,1,0:T(8,128)}), f32[8,224,128]{2,1,0:T(8,128)S(1)}, u32[]{:S(2)}, u32[]{:S(2)}) async-start(f32[8,224,128]{2,1,0:T(8,128)} %get-tuple-element.23), calls=%async_computation | async-start | bytes 1835008 | tf_op jit(solution)/shard_map/all_to_all | solution.py:272
  21.0 37.0 %copy-start.5 = (bf16[2,368,128]{2,1,0:T(8,128)(2,1)S(1)}, bf16[2,368,128]{2,1,0:T(8,128)(2,1)}, u32[]{:S(2)}) copy-start(bf16[2,368,128]{2,1,0:T(8,128)(2,1)} %cot_ref.1) | copy-start | bytes 565252
  21.0 105.3 %all-gather.7.cloned.1.call-start = ((), (), s32[]{:S(2)}) async-start(), calls=%async_computation.7 | async-start | bytes 2359296 | tf_op jit(solution)/shard_map/all_gather | solution.py:305
  21.0 0.8 collective-permute-start
  48.2 23.2 %all-to-all-start.2 = ((bf16[8,64,128]{2,1,0:T(8,128)(2,1)}), bf16[8,64,128]{2,1,0:T(8,128)(2,1)S(1)}, u32[]{:S(2)}, u32[]{:S(2)}) async-start(bf16[8,64,128]{2,1,0:T(8,128)(2,1)} %get-tuple-element.26), calls=%async_computation.2 | async-start | bytes 262144 | tf_op jit(solution)/shard_map/all_to_all | solution.py:272
  58.0 1.6 %copy-start = (bf16[1,2,4096,128]{3,2,1,0:T(8,128)(2,1)S(1)}, bf16[1,2,4096,128]{3,2,1,0:T(8,128)(2,1)}, u32[]{:S(2)}) copy-start(bf16[1,2,4096,128]{3,2,1,0:T(8,128)(2,1)} %param.8) | copy-start | bytes 6291460
  59.6 2.3 %copy-start.1 = (bf16[48,368,128]{2,1,0:T(8,128)(2,1)S(1)}, bf16[48,368,128]{2,1,0:T(8,128)(2,1)}, u32[]{:S(2)}) copy-start(bf16[48,368,128]{2,1,0:T(8,128)(2,1)} %all-gather.5.cloned.1.call-done) | copy-start | bytes 13565956
  63.3 1.3 copy-start.2
  90.3 33.4 %copy-start.3 = (bf16[2,4096,128]{2,1,0:T(8,128)(2,1)S(1)}, bf16[2,4096,128]{2,1,0:T(8,128)(2,1)}, u32[]{:S(2)}) copy-start(bf16[2,4096,128]{2,1,0:T(8,128)(2,1)} %copy-done.2) | copy-start | bytes 6291460
  126.3 1.6 %copy-start.6 = (bf16[64,128,128]{2,1,0:T(8,128)(2,1)S(1)}, bf16[64,128,128]{2,1,0:T(8,128)(2,1)}, u32[]{:S(2)}) copy-start(bf16[64,128,128]{2,1,0:T(8,128)(2,1)} %all-gather.7.cloned.1.call-done) | copy-start | bytes 6291460
  128.9 5.0 %collective-permute-start.1 = (bf16[368,512]{1,0:T(8,128)(2,1)S(1)}, bf16[368,512]{1,0:T(8,128)(2,1)S(1)}, u32[]{:S(2)}, u32[]{:S(2)}) collective-permute-start(bf16[368,512]{1,0:T(8,128)(2,1)S(1)} %get-tuple-element.32), channel_id=1, source_target_pairs={{0,1},{1,0},{2,3},{3,2},{4,5},{5,4},{6,7},{7,6},{8,9},{9,8},{10,11... | collective-permute-start | bytes 1130504 | tf_op jit(solution)/shard_map/ppermute | solution.py:348
Sparse Core Ops, SparseCore 0:
  10.7 46.8 all-gather.4
  60.3 65.3 all-gather.6
